TPU v7x, 256 devices: a whole 4x4x8 slice. The times are simulated.
256 devices in a mesh: gx: 16 (over y, z_lo), gy: 16 (over z_hi, x, core).
Axes of the slice: x: 4, y: 4, z: 8 (z_hi: 2, z_lo: 4; z = z_hi * 4 + z_lo), core: 2. Of those that a mesh axis runs over, the one named last changes fastest.
Arguments:
- latents: bfloat16 [16, 16, 512, 128], P('gx', 'gy'), may hold values from -6 to 6
- edge_latents: bfloat16 [16, 16, 4096, 128], P('gx', 'gy'), may hold values from -6 to 6
- senders: int32 [16, 16, 4096], P('gx', 'gy'), may hold values from 0 to 1663, as said below
- receivers: int32 [16, 16, 4096], P('gx', 'gy'), may hold values from 0 to 255
- ghost_rows: int32 [16, 16, 3, 3, 128], P('gx', 'gy'), may hold values from 0 to 511
- edge_count: int32 [16, 16], P('gx', 'gy'), may hold values from 1024 to 4096, as said below
- node_cotangent: bfloat16 [16, 16, 512, 128], P('gx', 'gy'), may hold values from -6 to 6
- edge_cotangent: bfloat16 [16, 16, 4096, 128], P('gx', 'gy'), may hold values from -6 to 6
- edge_first: bfloat16 [2, 384, 128], replicated, may hold values from -0.3125 to 0.3125
- edge_second: bfloat16 [2, 128, 128], replicated, may hold values from -0.5 to 0.5
- edge_scale: float32 [2, 128], replicated, may hold values from 0.5 to 1.5
- node_first: bfloat16 [2, 256, 128], replicated, may hold values from -0.375 to 0.375
- node_second: bfloat16 [2, 128, 128], replicated, may hold values from -0.5 to 0.5
- node_scale: float32 [2, 128], replicated, may hold values from 0.5 to 1.5
Outputs:
- nodes_out: bfloat16 [16, 16, 512, 128], P('gx', 'gy')
- edges_out: bfloat16 [16, 16, 4096, 128], P('gx', 'gy')
- latents_grad: float32 [16, 16, 512, 128], P('gx', 'gy')
- edge_latents_grad: float32 [16, 16, 4096, 128], P('gx', 'gy')
- edge_first_grad: float32 [2, 384, 128], replicated
- edge_second_grad: float32 [2, 128, 128], replicated
- edge_scale_grad: float32 [2, 128], replicated
- node_first_grad: float32 [2, 256, 128], replicated
- node_second_grad: float32 [2, 128, 128], replicated
- node_scale_grad: float32 [2, 128], replicated
Inputs may be any that keep to these rules, and one draw needn't show every extreme that they name: `senders`: rows 0 to 511 of the node table are the domain's particles; row 512 + k * 128 + j is ghost row j of slot k = 3 a + b, from the neighbour at offset (a - 1, b - 1); slot 4 is never named. `edge_count`: edge slots at positions below the count are live, later ones are padding.
All inputs are finite; a program needn't handle non-finite values.
Results may differ from a plain program's by a relative error of at most 0.02.
Values may be sent and summed in bfloat16 or wider, within the bound.
No kernel may reach another device: no remote copies, remote signals or barrier semaphores. Data moves between devices by JAX's collectives and lax.ppermute only.
A program may use at most 128 MiB of HBM per device.

v0:
```python
import jax
import jax.numpy as jnp
from jax import lax
from jax.sharding import PartitionSpec as P

L = 128
LAYERS = 2
TILE = 256
DEG = 8


epsilon = 1e-05


def extended(value, sides, width):
    for axis, dim in sides:
        devices, length = (lax.axis_size(axis), value.shape[dim])
        up = [(i, (i + 1) % devices) for i in range(devices - 1)]
        down = [(j, i) for i, j in up]
        last = lax.slice_in_dim(value, length - width, length, axis=dim)
        initial = lax.slice_in_dim(value, 0, width, axis=dim)
        before = lax.ppermute(last, axis, up)
        after = lax.ppermute(initial, axis, down)
        value = jnp.concatenate([before, value, after], axis=dim)
    return value


def normalize(values, gains):
    center = jnp.mean(values, axis=-1, keepdims=True)
    spread = jnp.mean(jnp.square(values - center), axis=-1, keepdims=True)
    return (values - center) * lax.rsqrt(spread + epsilon) * gains


def layer_update(node32, ghost32, edge32, sender_ids, receiver_ids, edge_total, params):
    edge_first, edge_second, edge_scale, node_first, node_second, node_scale = params
    blocks = sender_ids.shape[0] // TILE
    nodes_b = node32.astype(jnp.bfloat16)
    node_table = jnp.concatenate([node32, ghost32.reshape(-1, L)], axis=0)
    sender_rows = jnp.take(node_table, sender_ids, axis=0).astype(jnp.bfloat16)
    onehot = (
        receiver_ids.reshape(blocks, TILE)[:, :, None]
        == jnp.arange(TILE, dtype=jnp.int32)[None, None, :]
    ).astype(jnp.bfloat16)
    tile_rows = jnp.repeat(nodes_b.reshape(-1, TILE, L), DEG, axis=0)
    received = (
        jnp.einsum("bei,bil->bel", onehot, tile_rows, preferred_element_type=jnp.float32)
        .reshape(-1, L)
        .astype(jnp.bfloat16)
    )
    joined = jnp.concatenate([sender_rows, received, edge32.astype(jnp.bfloat16)], axis=1)
    edge_hidden = jax.nn.silu(
        jnp.dot(joined, edge_first.astype(jnp.bfloat16), preferred_element_type=jnp.float32)
    ).astype(jnp.bfloat16)
    live_mask = (jnp.arange(sender_ids.shape[0], dtype=jnp.int32) < edge_total).astype(jnp.float32)[
        :, None
    ]
    message = (
        normalize(
            jnp.dot(
                edge_hidden, edge_second.astype(jnp.bfloat16), preferred_element_type=jnp.float32
            ),
            edge_scale,
        )
        * live_mask
    )
    edge_next = (edge32 + message).astype(jnp.bfloat16)
    message_b = message.astype(jnp.bfloat16)
    summed = jnp.einsum(
        "bei,bel->bil",
        onehot,
        message_b.reshape(blocks, TILE, L),
        preferred_element_type=jnp.float32,
    )
    inbound = summed.reshape(-1, DEG, TILE, L).sum(axis=1).reshape(-1, L).astype(jnp.bfloat16)
    node_input = jnp.concatenate([nodes_b, inbound], axis=1)
    node_hidden = jax.nn.silu(
        jnp.dot(node_input, node_first.astype(jnp.bfloat16), preferred_element_type=jnp.float32)
    ).astype(jnp.bfloat16)
    update = normalize(
        jnp.dot(node_hidden, node_second.astype(jnp.bfloat16), preferred_element_type=jnp.float32),
        node_scale,
    )
    node_next = (node32 + update).astype(jnp.bfloat16)
    return (node_next, edge_next)


def outer_slots():
    return jnp.ones((3, 3), jnp.float32).at[1, 1].set(0.0)


def share_ghosts(nodes_b, ghost_ids):
    picked = jnp.take(nodes_b, ghost_ids, axis=0) * outer_slots()[:, :, None, None].astype(
        jnp.bfloat16
    )
    padded = extended(picked, (("gx", 0), ("gy", 1)), 1)
    return padded[::2, ::2]


def share_again(nodes_b, ghost_ids):
    picked = jnp.take(nodes_b, ghost_ids, axis=0) * outer_slots()[:, :, None, None].astype(
        jnp.bfloat16
    )
    padded = extended(picked, (("gx", 0), ("gy", 1)), 1)
    return padded[::2, ::2]


def return_grads(ghost_grad):
    padded = extended(ghost_grad.astype(jnp.bfloat16), (("gx", 0), ("gy", 1)), 1).astype(
        ghost_grad.dtype
    )
    return padded[::2, ::2] * outer_slots()[:, :, None, None]


def on_device(
    latents,
    edge_latents,
    senders,
    receivers,
    ghost_rows,
    edge_count,
    node_cotangent,
    edge_cotangent,
    edge_first,
    edge_second,
    edge_scale,
    node_first,
    node_second,
    node_scale,
):
    nodes_b = latents[0, 0]
    edges_b = edge_latents[0, 0]
    sender_ids = senders[0, 0]
    receiver_ids = receivers[0, 0]
    ghost_ids = ghost_rows[0, 0]
    edge_total = edge_count[0, 0]
    params32 = (
        edge_first.astype(jnp.float32),
        edge_second.astype(jnp.float32),
        edge_scale,
        node_first.astype(jnp.float32),
        node_second.astype(jnp.float32),
        node_scale,
    )
    layer_params = [
        tuple((weights[layer_index] for weights in params32)) for layer_index in range(LAYERS)
    ]

    def advance(node32, ghost32, edge32, weights):
        return layer_update(node32, ghost32, edge32, sender_ids, receiver_ids, edge_total, weights)

    stored_state = []
    for layer_index in range(LAYERS):
        ghost_slabs = share_ghosts(nodes_b, ghost_ids)
        ghosts = ghost_slabs.astype(jnp.float32)
        inputs = (
            nodes_b.astype(jnp.float32),
            ghosts,
            edges_b.astype(jnp.float32),
            layer_params[layer_index],
        )
        stored_state.append((nodes_b, edges_b))
        nodes_b, edges_b = advance(*inputs)
    node_grad = node_cotangent[0, 0]
    edge_grad = edge_cotangent[0, 0]
    node32_grad = None
    edge32_grad = None
    weight_grads = [None] * LAYERS
    for layer_index in reversed(range(LAYERS)):
        prior_nodes, prior_edges = stored_state[layer_index]
        ghosts = share_again(prior_nodes, ghost_ids).astype(jnp.float32)
        unused, pullback = jax.vjp(
            advance,
            prior_nodes.astype(jnp.float32),
            ghosts,
            prior_edges.astype(jnp.float32),
            layer_params[layer_index],
        )
        node32_grad, ghost_grad, edge32_grad, param_grad = pullback((node_grad, edge_grad))
        returned = return_grads(ghost_grad)
        node32_grad = node32_grad + jnp.zeros_like(node32_grad).at[ghost_ids.reshape(-1)].add(
            returned.reshape(-1, L)
        )
        param_grad = lax.psum(
            (
                param_grad[0],
                param_grad[1],
                param_grad[2],
                param_grad[3],
                param_grad[4],
                param_grad[5],
            ),
            ("gx", "gy"),
        )
        weight_grads[layer_index] = param_grad
        node_grad = node32_grad.astype(jnp.bfloat16)
        edge_grad = edge32_grad.astype(jnp.bfloat16)
    stacked = tuple(
        (jnp.stack([grads[position] for grads in weight_grads], axis=0) for position in range(6))
    )
    return (
        nodes_b[None, None],
        edges_b[None, None],
        node32_grad[None, None],
        edge32_grad[None, None],
        stacked[0],
        stacked[1],
        stacked[2],
        stacked[3],
        stacked[4],
        stacked[5],
    )


def solution(mesh):
    placed = (
        P("gx", "gy", None, None),
        P("gx", "gy", None, None),
        P("gx", "gy", None),
        P("gx", "gy", None),
        P("gx", "gy", None, None, None),
        P("gx", "gy"),
        P("gx", "gy", None, None),
        P("gx", "gy", None, None),
        P(),
        P(),
        P(),
        P(),
        P(),
        P(),
    )
    return jax.shard_map(
        on_device,
        mesh=mesh,
        in_specs=placed,
        out_specs=(
            P("gx", "gy", None, None),
            P("gx", "gy", None, None),
            P("gx", "gy", None, None),
            P("gx", "gy", None, None),
            P(),
            P(),
            P(),
            P(),
            P(),
            P(),
        ),
        check_vma=False,
    )
```

profile of v0, /device:TPU:1, one launch (start us, length us, event | category | flops | bytes accessed | tf_op | source)
XLA Modules:
  0.0 561.2 jit_solution(16849374172409918896)
XLA Ops:
  8.7 3.4 gather_fusion
  12.5 4.4 collective-permute-start
  16.9 1.3 collective-permute-start.1
  22.0 1.3 fusion.33
  23.4 1.5 collective-permute-done.1
  25.0 3.5 collective-permute-start.2
  28.5 1.9 collective-permute-start.3
  31.6 3.5 collective-permute-done.3
  35.3 12.1 %gather_fusion.1 = bf16[4096,128]{1,0:T(8,128)(2,1)S(1)} fusion(bf16[1664,128]{1,0:T(8,128)(2,1)S(1)} %pad_maximum_fusion.18, s32[4096]{0:T(1024)S(1)} %get-tuple-element.118), kind=kCustom, calls=%fused_computation.1.clone | custom fusion | bytes 2113536 | tf_op jit(solution)/shard_map/jit(_take)/gather | solution.py:39
  47.5 2.1 select_convert_fusion.1
  52.0 1.3 multiply_reduce_fusion.6
  53.4 3.7 fusion.31
  60.1 2.9 gather_fusion.2
  64.0 3.2 collective-permute-start.4
  67.2 1.3 collective-permute-start.5
  68.7 2.3 fusion.34
  71.2 1.5 collective-permute-done.5
  72.8 3.4 collective-permute-start.6
  76.2 2.1 collective-permute-start.7
  78.9 4.8 collective-permute-done.7
  83.9 15.0 %gather_fusion.3 = bf16[4096,128]{1,0:T(8,128)(2,1)} fusion(bf16[1664,128]{1,0:T(8,128)(2,1)S(1)} %pad_maximum_fusion.19, s32[4096]{0:T(1024)S(1)} %get-tuple-element.118), kind=kCustom, calls=%fused_computation.4.clone | custom fusion | bytes 2113536 | tf_op jit(solution)/shard_map/jit(_take)/gather | solution.py:39
  98.9 3.5 select_convert_fusion
  104.8 1.3 copy-done.2
  106.2 1.3 multiply_reduce_fusion.5
  107.5 3.6 fusion.32
  114.4 1.4 fusion.88
  118.5 2.9 multiply_reduce_fusion.3
  121.5 3.9 multiply_reduce_fusion
  125.4 2.0 multiply_reduce_fusion.9
  127.4 4.1 add_add_fusion.1
  131.5 1.4 fusion.59
  134.5 1.7 fusion.49
  137.2 1.6 copy-done.4
  138.8 23.7 %scatter_custom_fusion = f32[1664,128]{1,0:T(8,128)} fusion(s32[4096]{0:T(1024)} %get-tuple-element.117, bf16[4096,384]{1,0:T(8,128)(2,1)} %copy-done.4, f32[]{:T(128)} %constant.196.clone.1), kind=kCustom, calls=%fused_computation.51 | custom fusion | flops 1048576 | bytes 1901056 | tf_op jit(solution)/shard_map/transpose(jvp(jit(_take)))/scatter-add | solution.py:39
  162.5 1.2 convert.25
  163.8 1.4 collective-permute-start.9
  165.2 6.0 %collective-permute-start.8 = (bf16[1,3,128,128]{3,2,1,0:T(8,128)(2,1)S(1)}, bf16[1,3,128,128]{3,2,1,0:T(8,128)(2,1)S(1)}, u32[]{:S(2)}, u32[]{:S(2)}) collective-permute-start(bf16[1,3,128,128]{3,2,1,0:T(8,128)(2,1)S(1)} %bitcast.279), channel_id=1, source_target_pairs={{0,16},{16,32},{32,48},{48,64},{64,80},{80,96},{96,112},{112,128},... | collective-permute-start | bytes 294920 | tf_op jit(solution)/shard_map/ppermute | solution.py:22
  171.3 1.5 bitcast_reduce_fusion.3
  173.9 1.1 fusion.63
  175.2 2.0 collective-permute-start.10
  177.2 2.3 collective-permute-start.11
  180.5 3.3 collective-permute-done.11
  184.1 9.5 %scatter_fusion = f32[512,128]{1,0:T(8,128)S(1)} fusion(f32[512,128]{1,0:T(8,128)S(1)} %fusion.87, s32[1152]{0:T(1024)} %fusion.135, f32[1152,128]{1,0:T(8,128)S(1)} %bitcast.258), kind=kCustom, calls=%fused_computation.7 | custom fusion | flops 147456 | bytes 1774080 | tf_op jit(solution)/shard_map/scatter-add | solution.py:180
  195.0 1.4 fusion.86
  198.1 1.3 fusion.39
  199.7 3.8 multiply_reduce_fusion.1
  203.5 2.0 multiply_reduce_fusion.7
  205.5 3.8 add_add_fusion
  209.3 1.4 fusion.57
  212.6 1.7 fusion.51
  215.3 23.4 %scatter_custom_fusion.2 = f32[1664,128]{1,0:T(8,128)} fusion(s32[4096]{0:T(1024)} %get-tuple-element.117, bf16[4096,384]{1,0:T(8,128)(2,1)S(1)} %convolution_convert_fusion, f32[]{:T(128)} %constant.196.clone.1), kind=kCustom, calls=%fused_computation.47 | custom fusion | flops 1048576 | bytes 1901056 | tf_op jit(solution)/shard_map/transpose(jvp(jit(_take)))/scatter-add | solution.py:39
  238.8 2.7 fusion.11
  241.6 1.1 copy-done.9
  242.8 1.4 collective-permute-start.13
  244.2 4.3 collective-permute-start.12
  249.5 1.2 fusion.61
  250.8 2.0 collective-permute-start.14
  252.8 2.5 collective-permute-start.15
  256.3 111.8 %all-reduce = (f32[1,128]{1,0:T(1,128)S(1)}, f32[1,128]{1,0:T(1,128)S(1)}, f32[1,128]{1,0:T(1,128)S(1)}, f32[1,128]{1,0:T(1,128)S(1)}) all-reduce(f32[1,128]{1,0:T(1,128)S(1)} %bitcast.286, f32[1,128]{1,0:T(1,128)S(1)} %bitcast.289, f32[1,128]{1,0:T(1,128)S(1)} %bitcast.287, ...), channel_id=1, replica_groups=mesh['gx'=16,'gy'=16] {'gx','gy'}, use_global_device_ids=true, to_apply=%region_45.49 | all-reduce | flops 512 | bytes 4096 | tf_op jit(solution)/shard_map/psum | solution.py:183
  368.9 9.0 %scatter_fusion.1 = f32[512,128]{1,0:T(8,128)S(1)} fusion(f32[512,128]{1,0:T(8,128)S(1)} %fusion.83, s32[1152]{0:T(1024)S(1)} %copy-done.52, f32[1152,128]{1,0:T(8,128)S(1)} %bitcast.257), kind=kCustom, calls=%fused_computation.9 | custom fusion | flops 147456 | bytes 1774080 | tf_op jit(solution)/shard_map/scatter-add | solution.py:180
  377.9 171.1 %all-reduce.4.cloned.1.call-done = (f32[1,384,128]{2,1,0:T(8,128)}, f32[1,384,128]{2,1,0:T(8,128)}, f32[1,128,128]{2,1,0:T(8,128)}, f32[1,128,128]{2,1,0:T(8,128...) async-done(((f32[1,384,128]{2,1,0:T(8,128)}, f32[1,384,128]{2,1,0:T(8,128)}, f32[1,128,128]{2,1,0:T(8,128)}, ...) | async-done | bytes 917520 | tf_op jit(solution)/shard_map/psum | solution.py:183
  549.0 1.8 pad_maximum_fusion.24
  550.8 1.7 pad_maximum_fusion.27
  552.5 1.6 pad_maximum_fusion.44
  (342 shorter events, 35.7 us)
Async XLA Ops:
  7.2 5.0 copy-start.90
  7.2 14.6 %copy-start.1 = (bf16[1,1,512,128]{3,2,1,0:T(8,128)(2,1)S(1)}, bf16[1,1,512,128]{3,2,1,0:T(8,128)(2,1)}, u32[]{:S(2)}) copy-start(bf16[1,1,512,128]{3,2,1,0:T(8,128)(2,1)} %param.32) | copy-start | bytes 393220
  7.2 11.0 %copy-start.53 = (s32[1,1,4096]{2,1,0:T(1,128)S(1)}, s32[1,1,4096]{2,1,0:T(1,128)}, u32[]{:S(2)}) copy-start(s32[1,1,4096]{2,1,0:T(1,128)} %param.34) | copy-start | bytes 49156
  7.2 12.2 %copy-start.101 = (f32[2,128]{1,0:T(2,128)S(1)}, f32[2,128]{1,0:T(2,128)}, u32[]{:S(2)}) copy-start(f32[2,128]{1,0:T(2,128)} %param.42) | copy-start | bytes 3076
  7.2 12.8 %copy-start.102 = (f32[2,128]{1,0:T(2,128)S(1)}, f32[2,128]{1,0:T(2,128)}, u32[]{:S(2)}) copy-start(f32[2,128]{1,0:T(2,128)} %param.45) | copy-start | bytes 3076
  7.2 13.9 %copy-start.66 = (s32[1,1,4096]{2,1,0:T(1,128)S(1)}, s32[1,1,4096]{2,1,0:T(1,128)}, u32[]{:S(2)}) copy-start(s32[1,1,4096]{2,1,0:T(1,128)} %param.35) | copy-start | bytes 49156
  7.2 541.8 %all-reduce.4.cloned.1.call-start = ((), (), s32[]{:S(2)}) async-start(), calls=%async_computation | async-start | bytes 1835008 | tf_op jit(solution)/shard_map/psum | solution.py:183
  8.0 4.2 copy-start.73
  12.5 10.9 %collective-permute-start = (bf16[1,3,128,128]{3,2,1,0:T(8,128)(2,1)S(1)}, bf16[1,3,128,128]{3,2,1,0:T(8,128)(2,1)S(1)}, u32[]{:S(2)}, u32[]{:S(2)}) collective-permute-start(bf16[1,3,128,128]{3,2,1,0:T(8,128)(2,1)S(1)} %get-tuple-element.114), channel_id=1, source_target_pairs={{0,16},{16,32},{32,48},{48,64},{64,80},{80,96},{96,112},{112,128},... | collective-permute-start | bytes 294920 | tf_op jit(solution)/shard_map/ppermute | solution.py:22
  16.9 8.1 %collective-permute-start.1 = (bf16[1,3,128,128]{3,2,1,0:T(8,128)(2,1)S(1)}, bf16[1,3,128,128]{3,2,1,0:T(8,128)(2,1)S(1)}, u32[]{:S(2)}, u32[]{:S(2)}) collective-permute-start(bf16[1,3,128,128]{3,2,1,0:T(8,128)(2,1)S(1)} %get-tuple-element.115), channel_id=1, source_target_pairs={{16,0},{32,16},{48,32},{64,48},{80,64},{96,80},{112,96},{128,112},... | collective-permute-start | bytes 294920 | tf_op jit(solution)/shard_map/ppermute | solution.py:23
  18.2 29.3 %copy-start.57 = (pred[4096]{0:T(1024)(128)(4,1)}, pred[4096]{0:T(1024)(128)(4,1)S(1)}, u32[]{:S(2)}) copy-start(pred[4096]{0:T(1024)(128)(4,1)S(1)} %compare_and_fusion) | copy-start | bytes 12292
  20.0 33.4 %copy-start.85 = (f32[128]{0:T(128)}, f32[128]{0:T(128)S(1)}, u32[]{:S(2)}) copy-start(f32[128]{0:T(128)S(1)} %get-tuple-element.122) | copy-start | bytes 1540
  20.6 39.3 %copy-start.87 = (f32[128]{0:T(128)}, f32[128]{0:T(128)S(1)}, u32[]{:S(2)}) copy-start(f32[128]{0:T(128)S(1)} %get-tuple-element.120) | copy-start | bytes 1540
  21.8 35.3 %copy-start.67 = (s32[16,256]{1,0:T(8,128)}, s32[16,256]{1,0:T(8,128)S(1)}, u32[]{:S(2)}) copy-start(s32[16,256]{1,0:T(8,128)S(1)} %eq.8) | copy-start | bytes 49156
  22.0 9.0 %copy-start.56 = (s32[1,1,3,3,128]{4,1,3,2,0:T(1,128)S(1)}, s32[1,1,3,3,128]{4,1,3,2,0:T(1,128)}, u32[]{:S(2)}) copy-start(s32[1,1,3,3,128]{4,1,3,2,0:T(1,128)} %param.36) | copy-start | bytes 13828
  23.3 26.3 %copy-start.108 = (bf16[16,256,128]{2,1,0:T(8,128)(2,1)}, bf16[16,256,128]{2,1,0:T(8,128)(2,1)S(1)}, u32[]{:S(2)}) copy-start(bf16[16,256,128]{2,1,0:T(8,128)(2,1)S(1)} %fusion.33) | copy-start | bytes 3145732
  25.0 6.7 %collective-permute-start.2 = (bf16[5,1,128,128]{3,2,1,0:T(8,128)(2,1)S(1)}, bf16[5,1,128,128]{3,2,1,0:T(8,128)(2,1)S(1)}, u32[]{:S(2)}, u32[]{:S(2)}) collective-permute-start(bf16[5,1,128,128]{3,2,1,0:T(8,128)(2,1)S(1)} %get-tuple-element.106), channel_id=1, source_target_pairs={{0,1},{1,2},{2,3},{3,4},{4,5},{5,6},{6,7},{7,8},{8,9},{9,10},{10,1... | collective-permute-start | bytes 491528 | tf_op jit(solution)/shard_map/ppermute | solution.py:22
  28.5 6.6 %collective-permute-start.3 = (bf16[5,1,128,128]{3,2,1,0:T(8,128)(2,1)S(1)}, bf16[5,1,128,128]{3,2,1,0:T(8,128)(2,1)S(1)}, u32[]{:S(2)}, u32[]{:S(2)}) collective-permute-start(bf16[5,1,128,128]{3,2,1,0:T(8,128)(2,1)S(1)} %get-tuple-element.107), channel_id=1, source_target_pairs={{1,0},{2,1},{3,2},{4,3},{5,4},{6,5},{7,6},{8,7},{9,8},{10,9},{11,1... | collective-permute-start | bytes 491528 | tf_op jit(solution)/shard_map/ppermute | solution.py:23
  52.0 5.0 copy-start.26
  59.4 11.6 %copy-start.59 = (f32[512]{0:T(512)}, f32[512]{0:T(512)S(1)}, u32[]{:S(2)}) copy-start(f32[512]{0:T(512)S(1)} %broadcast_multiply_fusion.2) | copy-start | bytes 6148
  59.6 11.4 %copy-start.10 = (f32[512,128]{1,0:T(8,128)}, f32[512,128]{1,0:T(8,128)S(1)}, u32[]{:S(2)}) copy-start(f32[512,128]{1,0:T(8,128)S(1)} %copy.36) | copy-start | bytes 786436
  60.1 8.6 %copy-start.68 = (s32[16,256]{1,0:T(8,128)S(1)}, s32[16,256]{1,0:T(8,128)}, u32[]{:S(2)}) copy-start(s32[16,256]{1,0:T(8,128)} %copy-done.67) | copy-start | bytes 49156
  64.0 7.3 %collective-permute-start.4 = (bf16[1,3,128,128]{3,2,1,0:T(8,128)(2,1)S(1)}, bf16[1,3,128,128]{3,2,1,0:T(8,128)(2,1)S(1)}, u32[]{:S(2)}, u32[]{:S(2)}) collective-permute-start(bf16[1,3,128,128]{3,2,1,0:T(8,128)(2,1)S(1)} %get-tuple-element.112), channel_id=1, source_target_pairs={{0,16},{16,32},{32,48},{48,64},{64,80},{80,96},{96,112},{112,128},... | collective-permute-start | bytes 294920 | tf_op jit(solution)/shard_map/ppermute | solution.py:22
  67.2 5.6 collective-permute-start.5
  71.2 27.7 %copy-start.64 = (f32[512]{0:T(512)}, f32[512]{0:T(512)S(1)}, u32[]{:S(2)}) copy-start(f32[512]{0:T(512)S(1)} %multiply_reduce_fusion.10) | copy-start | bytes 6148
  72.8 6.1 %collective-permute-start.6 = (bf16[5,1,128,128]{3,2,1,0:T(8,128)(2,1)S(1)}, bf16[5,1,128,128]{3,2,1,0:T(8,128)(2,1)S(1)}, u32[]{:S(2)}, u32[]{:S(2)}) collective-permute-start(bf16[5,1,128,128]{3,2,1,0:T(8,128)(2,1)S(1)} %get-tuple-element.104), channel_id=1, source_target_pairs={{0,1},{1,2},{2,3},{3,4},{4,5},{5,6},{6,7},{7,8},{8,9},{9,10},{10,1... | collective-permute-start | bytes 491528 | tf_op jit(solution)/shard_map/ppermute | solution.py:22
  76.2 7.5 %collective-permute-start.7 = (bf16[5,1,128,128]{3,2,1,0:T(8,128)(2,1)S(1)}, bf16[5,1,128,128]{3,2,1,0:T(8,128)(2,1)S(1)}, u32[]{:S(2)}, u32[]{:S(2)}) collective-permute-start(bf16[5,1,128,128]{3,2,1,0:T(8,128)(2,1)S(1)} %get-tuple-element.105), channel_id=1, source_target_pairs={{1,0},{2,1},{3,2},{4,3},{5,4},{6,5},{7,6},{8,7},{9,8},{10,9},{11,1... | collective-permute-start | bytes 491528 | tf_op jit(solution)/shard_map/ppermute | solution.py:23
  83.8 15.1 %copy-start.58 = (pred[4096]{0:T(1024)(128)(4,1)S(1)}, pred[4096]{0:T(1024)(128)(4,1)}, u32[]{:S(2)}) copy-start(pred[4096]{0:T(1024)(128)(4,1)} %copy-done.57) | copy-start | bytes 12292
  111.8 4.3 copy-start.50
  112.1 4.5 copy-start.37
  113.0 4.5 copy-start.62
  114.1 4.3 copy-start.12
  116.2 5.3 copy-start.92
  138.8 32.4 %slice-start = ((bf16[4096,384]{1,0:T(8,128)(2,1)}), bf16[4096,128]{1,0:T(8,128)(2,1)S(1)}, s32[]{:S(2)}) async-start(bf16[4096,384]{1,0:T(8,128)(2,1)} %copy-done.4), calls=%async_computation.1 | async-start | bytes 2097152 | tf_op jit(solution)/shard_map/transpose(jvp())/split | solution.py:50
  163.7 9.1 %copy-start.17 = (bf16[512,256]{1,0:T(8,128)(2,1)S(1)}, bf16[512,256]{1,0:T(8,128)(2,1)}, u32[]{:S(2)}) copy-start(bf16[512,256]{1,0:T(8,128)(2,1)} %copy-done.16) | copy-start | bytes 786436
  163.8 11.4 %collective-permute-start.9 = (bf16[1,3,128,128]{3,2,1,0:T(8,128)(2,1)S(1)}, bf16[1,3,128,128]{3,2,1,0:T(8,128)(2,1)S(1)}, u32[]{:S(2)}, u32[]{:S(2)}) collective-permute-start(bf16[1,3,128,128]{3,2,1,0:T(8,128)(2,1)S(1)} %bitcast.281), channel_id=1, source_target_pairs={{16,0},{32,16},{48,32},{64,48},{80,64},{96,80},{112,96},{128,112},... | collective-permute-start | bytes 294920 | tf_op jit(solution)/shard_map/ppermute | solution.py:23
  165.2 9.9 %collective-permute-start.8 = (bf16[1,3,128,128]{3,2,1,0:T(8,128)(2,1)S(1)}, bf16[1,3,128,128]{3,2,1,0:T(8,128)(2,1)S(1)}, u32[]{:S(2)}, u32[]{:S(2)}) collective-permute-start(bf16[1,3,128,128]{3,2,1,0:T(8,128)(2,1)S(1)} %bitcast.279), channel_id=1, source_target_pairs={{0,16},{16,32},{32,48},{48,64},{64,80},{80,96},{96,112},{112,128},... | collective-permute-start | bytes 294920 | tf_op jit(solution)/shard_map/ppermute | solution.py:22
  172.8 6.7 %copy-start.45 = (bf16[512,128]{1,0:T(8,128)(2,1)S(1)}, bf16[512,128]{1,0:T(8,128)(2,1)}, u32[]{:S(2)}) copy-start(bf16[512,128]{1,0:T(8,128)(2,1)} %copy-done.44) | copy-start | bytes 393220
  172.8 6.7 %copy-start.51 = (bf16[2,256,128]{2,1,0:T(8,128)(2,1)S(1)}, bf16[2,256,128]{2,1,0:T(8,128)(2,1)}, u32[]{:S(2)}) copy-start(bf16[2,256,128]{2,1,0:T(8,128)(2,1)} %copy-done.50) | copy-start | bytes 393220
  175.1 8.9 %copy-start.74 = (f32[3,3]{1,0:T(4,128)S(1)}, f32[3,3]{1,0:T(4,128)}, u32[]{:S(2)}) copy-start(f32[3,3]{1,0:T(4,128)} %constant.205.clone.1) | copy-start | bytes 112
  175.2 5.3 collective-permute-start.10
  177.2 6.6 %collective-permute-start.11 = (bf16[5,1,128,128]{3,2,1,0:T(8,128)(2,1)S(1)}, bf16[5,1,128,128]{3,2,1,0:T(8,128)(2,1)S(1)}, u32[]{:S(2)}, u32[]{:S(2)}) collective-permute-start(bf16[5,1,128,128]{3,2,1,0:T(8,128)(2,1)S(1)} %get-tuple-element.103), channel_id=1, source_target_pairs={{1,0},{2,1},{3,2},{4,3},{5,4},{6,5},{7,6},{8,7},{9,8},{10,9},{11,1... | collective-permute-start | bytes 491528 | tf_op jit(solution)/shard_map/ppermute | solution.py:23
  184.1 9.6 %copy-start.11 = (f32[512,128]{1,0:T(8,128)S(1)}, f32[512,128]{1,0:T(8,128)}, u32[]{:S(2)}) copy-start(f32[512,128]{1,0:T(8,128)} %copy-done.10) | copy-start | bytes 786436
  184.1 9.6 %copy-start.60 = (f32[512]{0:T(512)S(1)}, f32[512]{0:T(512)}, u32[]{:S(2)}) copy-start(f32[512]{0:T(512)} %copy-done.59) | copy-start | bytes 6148
  184.1 9.6 %copy-start.80 = (f32[512]{0:T(512)S(1)}, f32[512]{0:T(512)}, u32[]{:S(2)}) copy-start(f32[512]{0:T(512)} %fusion.137) | copy-start | bytes 6148
  184.1 9.6 %copy-start.88 = (f32[128]{0:T(128)S(1)}, f32[128]{0:T(128)}, u32[]{:S(2)}) copy-start(f32[128]{0:T(128)} %copy-done.87) | copy-start | bytes 1540
  184.1 10.3 %copy-start.65 = (f32[512]{0:T(512)S(1)}, f32[512]{0:T(512)}, u32[]{:S(2)}) copy-start(f32[512]{0:T(512)} %copy-done.64) | copy-start | bytes 6148
  203.5 5.8 %copy-start.8 = (bf16[4096,128]{1,0:T(8,128)(2,1)}, bf16[4096,128]{1,0:T(8,128)(2,1)S(1)}, u32[]{:S(2)}) copy-start(bf16[4096,128]{1,0:T(8,128)(2,1)S(1)} %get-tuple-element.95) | copy-start | bytes 3145732
  241.5 7.0 %copy-start.71 = (s32[16,256]{1,0:T(8,128)S(1)}, s32[16,256]{1,0:T(8,128)}, u32[]{:S(2)}) copy-start(s32[16,256]{1,0:T(8,128)} %copy-done.67) | copy-start | bytes 49156
  242.7 6.5 %copy-start.19 = (bf16[512,256]{1,0:T(8,128)(2,1)S(1)}, bf16[512,256]{1,0:T(8,128)(2,1)}, u32[]{:S(2)}) copy-start(bf16[512,256]{1,0:T(8,128)(2,1)} %copy-done.18) | copy-start | bytes 786436
  242.7 6.5 %copy-start.32 = (bf16[512,128]{1,0:T(8,128)(2,1)S(1)}, bf16[512,128]{1,0:T(8,128)(2,1)}, u32[]{:S(2)}) copy-start(bf16[512,128]{1,0:T(8,128)(2,1)} %copy-done.31) | copy-start | bytes 393220
  242.8 7.9 %collective-permute-start.13 = (bf16[1,3,128,128]{3,2,1,0:T(8,128)(2,1)S(1)}, bf16[1,3,128,128]{3,2,1,0:T(8,128)(2,1)S(1)}, u32[]{:S(2)}, u32[]{:S(2)}) collective-permute-start(bf16[1,3,128,128]{3,2,1,0:T(8,128)(2,1)S(1)} %bitcast.280), channel_id=1, source_target_pairs={{16,0},{32,16},{48,32},{64,48},{80,64},{96,80},{112,96},{128,112},... | collective-permute-start | bytes 294920 | tf_op jit(solution)/shard_map/ppermute | solution.py:23
  244.2 6.5 %collective-permute-start.12 = (bf16[1,3,128,128]{3,2,1,0:T(8,128)(2,1)S(1)}, bf16[1,3,128,128]{3,2,1,0:T(8,128)(2,1)S(1)}, u32[]{:S(2)}, u32[]{:S(2)}) collective-permute-start(bf16[1,3,128,128]{3,2,1,0:T(8,128)(2,1)S(1)} %bitcast.278), channel_id=1, source_target_pairs={{0,16},{16,32},{32,48},{48,64},{64,80},{80,96},{96,112},{112,128},... | collective-permute-start | bytes 294920 | tf_op jit(solution)/shard_map/ppermute | solution.py:22
  249.3 6.0 %copy-start.47 = (bf16[512,128]{1,0:T(8,128)(2,1)S(1)}, bf16[512,128]{1,0:T(8,128)(2,1)}, u32[]{:S(2)}) copy-start(bf16[512,128]{1,0:T(8,128)(2,1)} %copy-done.46) | copy-start | bytes 393220
  249.3 6.0 %copy-start.49 = (bf16[2,256,128]{2,1,0:T(8,128)(2,1)S(1)}, bf16[2,256,128]{2,1,0:T(8,128)(2,1)}, u32[]{:S(2)}) copy-start(bf16[2,256,128]{2,1,0:T(8,128)(2,1)} %copy-done.48) | copy-start | bytes 393220
  249.5 6.8 %copy-start.91 = (f32[128]{0:T(128)S(1)}, f32[128]{0:T(128)}, u32[]{:S(2)}) copy-start(f32[128]{0:T(128)} %get-tuple-element.72) | copy-start | bytes 1540
  249.5 6.8 %copy-start.98 = (f32[128]{0:T(128)S(1)}, f32[128]{0:T(128)}, u32[]{:S(2)}) copy-start(f32[128]{0:T(128)} %get-tuple-element.79) | copy-start | bytes 1540
  249.5 6.8 %copy-start.99 = (f32[128]{0:T(128)S(1)}, f32[128]{0:T(128)}, u32[]{:S(2)}) copy-start(f32[128]{0:T(128)} %get-tuple-element.77) | copy-start | bytes 1540
  249.5 6.8 %copy-start.100 = (f32[128]{0:T(128)S(1)}, f32[128]{0:T(128)}, u32[]{:S(2)}) copy-start(f32[128]{0:T(128)} %get-tuple-element.74) | copy-start | bytes 1540
  250.7 118.1 %copy-start.75 = (f32[3,3]{1,0:T(4,128)S(1)}, f32[3,3]{1,0:T(4,128)}, u32[]{:S(2)}) copy-start(f32[3,3]{1,0:T(4,128)} %constant.205.clone.1) | copy-start | bytes 112
  250.8 118.2 %copy-start.52 = (s32[1152]{0:T(1024)S(1)}, s32[1152]{0:T(1024)}, u32[]{:S(2)}) copy-start(s32[1152]{0:T(1024)} %fusion.135) | copy-start | bytes 13828
  250.8 117.9 %collective-permute-start.14 = (bf16[5,1,128,128]{3,2,1,0:T(8,128)(2,1)S(1)}, bf16[5,1,128,128]{3,2,1,0:T(8,128)(2,1)S(1)}, u32[]{:S(2)}, u32[]{:S(2)}) collective-permute-start(bf16[5,1,128,128]{3,2,1,0:T(8,128)(2,1)S(1)} %get-tuple-element.100), channel_id=1, source_target_pairs={{0,1},{1,2},{2,3},{3,4},{4,5},{5,6},{6,7},{7,8},{8,9},{9,10},{10,1... | collective-permute-start | bytes 491528 | tf_op jit(solution)/shard_map/ppermute | solution.py:22
  252.8 115.8 %collective-permute-start.15 = (bf16[5,1,128,128]{3,2,1,0:T(8,128)(2,1)S(1)}, bf16[5,1,128,128]{3,2,1,0:T(8,128)(2,1)S(1)}, u32[]{:S(2)}, u32[]{:S(2)}) collective-permute-start(bf16[5,1,128,128]{3,2,1,0:T(8,128)(2,1)S(1)} %get-tuple-element.101), channel_id=1, source_target_pairs={{1,0},{2,1},{3,2},{4,3},{5,4},{6,5},{7,6},{8,7},{9,8},{10,9},{11,1... | collective-permute-start | bytes 491528 | tf_op jit(solution)/shard_map/ppermute | solution.py:23
  377.9 176.2 %copy-start = (f32[512,128]{1,0:T(8,128)}, f32[512,128]{1,0:T(8,128)S(1)}, u32[]{:S(2)}) copy-start(f32[512,128]{1,0:T(8,128)S(1)} %scatter_fusion.1) | copy-start | bytes 786436
  (70 other events, 144.6 us)
Sparse Core Ops, SparseCore 0:
  256.4 292.5 all-reduce.3
where the time goes:
time: 570 us; the launch traced here: 561 us
  waiting for transfers between devices  186 us (33%)
  other arithmetic  122 us (21%)
  blocking collectives  112 us (20%)
  local copies, waits for them, and re-layouts  48.1 us (8%)
  starting transfers between devices  43 us (8%)
  matrix products  33.6 us (6%)
  between operations  17 us (3%)
    psum x1, waiting for transfers between devices, on_device(): lax.psum((param_grad[0], param_grad[1], param_grad[2], param_grad[3], par...  171 us
    psum x1, blocking collectives, on_device(): lax.psum((param_grad[0], param_grad[1], param_grad[2], param_grad[3], par...  112 us
    scatter-add x2, other arithmetic, layer_update(): sender_rows = jnp.take(node_table, sender_ids, axis=0).astype(jnp.bfloat16)  47.2 us
    ppermute x8, starting transfers between devices, extended(): before = lax.ppermute(last, axis, up)  28.8 us
    gather x2, local copies, waits for them, and re-layouts, layer_update(): sender_rows = jnp.take(node_table, sender_ids, axis=0).astype(jnp.bfloat16)  27.2 us
    scatter-add x2, other arithmetic, on_device(): jnp.zeros_like(node32_grad).at[ghost_ids.reshape(-1)]  18.5 us
    ppermute x8, waiting for transfers between devices, extended(): after = lax.ppermute(initial, axis, down)  14.7 us
    ppermute x8, starting transfers between devices, extended(): after = lax.ppermute(initial, axis, down)  14.2 us
  transfers between devices with their start and end apart: 17, of which 6 were waited for; matrix products, arithmetic and copies ran while one was open for 5% of the time, Pallas kernels for 0%

commit v1 on v0

v1 whole, which is shorter than its diff:
```python
import jax
import jax.numpy as jnp
from jax import lax
from jax.experimental import pallas as pl
from jax.experimental.pallas import tpu as pltpu
from jax.sharding import PartitionSpec as P

L = 128
LAYERS = 2
TILE = 256
DEG = 8
SLOTS = 8
G = 128
NODES = 512
EDGES = 4096
GHOSTS = SLOTS * G
HALF = (NODES + GHOSTS) // 2
BLOCK = 512
BLOCKS = EDGES // BLOCK
PER_TILE = TILE * DEG // BLOCK
PACKED = 1024

F32 = jnp.float32
BF16 = jnp.bfloat16
epsilon = 1e-05


def dot(a, b):
    return jnp.dot(a, b, preferred_element_type=F32)


def dot_nt(a, b):
    return lax.dot_general(a, b, (((1,), (1,)), ((), ())), preferred_element_type=F32)


def dot_tn(a, b):
    return lax.dot_general(a, b, (((0,), (0,)), ((), ())), preferred_element_type=F32)


def sigmoid(v):
    return 1.0 / (1.0 + jnp.exp(-v))


def column(rows, count):
    parts = [
        jnp.transpose(jnp.broadcast_to(rows[i : i + 1, :], (128, 128))) for i in range(count)
    ]
    return jnp.concatenate(parts, axis=0) if count > 1 else parts[0]


def flat_row(rows, count):
    parts = [rows[i : i + 1, :] for i in range(count)]
    return jnp.concatenate(parts, axis=1) if count > 1 else parts[0]


def hits(col, width):
    lane = lax.broadcasted_iota(jnp.int32, col.shape, 1).astype(F32)
    parts = [
        jnp.where(col == lane + float(128 * t), 1.0, 0.0).astype(BF16) for t in range(width // 128)
    ]
    return jnp.concatenate(parts, axis=1)


def hits_t(row, height):
    sub = lax.broadcasted_iota(jnp.int32, (height, row.shape[1]), 0).astype(F32)
    return jnp.where(sub == row, 1.0, 0.0).astype(BF16)


def layer_norm(y):
    center = y - jnp.mean(y, axis=-1, keepdims=True)
    spread = jnp.mean(center * center, axis=-1, keepdims=True)
    rstd = lax.rsqrt(spread + epsilon)
    return center * rstd, rstd


def layer_norm_grad(dn, n, rstd):
    return rstd * (
        dn
        - jnp.mean(dn, axis=-1, keepdims=True)
        - n * jnp.mean(dn * n, axis=-1, keepdims=True)
    )


def silu_grad(z):
    s = sigmoid(z)
    return s * (1.0 + z * (1.0 - s))


def pick(nodes_b, ghost_row_ref, out_ref):
    for s in range(SLOTS):
        col = column(ghost_row_ref[s : s + 1, :], 1)
        out_ref[pl.ds(s * G, G), :] = dot(hits(col, NODES), nodes_b).astype(BF16)


def build_table(nodes_ref, ghosts_ref, table):
    table[0:NODES, 0:L] = nodes_ref[...]
    table[NODES:HALF, 0:L] = ghosts_ref[0 : HALF - NODES, :]
    table[:, L : 2 * L] = ghosts_ref[HALF - NODES :, :]


def block_rows(ref, b):
    count = BLOCK // 128
    return ref[pl.ds(b * count, count), :]


def send_gather(b, srow_ref, table):
    col = column(block_rows(srow_ref, b), BLOCK // 128)
    upper = col >= float(HALF)
    both = dot(hits(jnp.where(upper, col - float(HALF), col), HALF), table[...])
    return jnp.where(upper, both[:, L:], both[:, :L]).astype(BF16)


def receive_hits(b, rrow_ref):
    return hits(column(block_rows(rrow_ref, b), BLOCK // 128), TILE)


def tile_of(b):
    return pl.ds(pl.multiple_of((b // PER_TILE) * TILE, TILE), TILE)


def block_of(b):
    return pl.ds(pl.multiple_of(b * BLOCK, BLOCK), BLOCK)


def live_of(b, count):
    slot = lax.broadcasted_iota(jnp.int32, (BLOCK, L), 0) + b * BLOCK
    return jnp.where(slot < count, 1.0, 0.0)


def edge_hidden(sent, received, edges_b, w1_ref):
    joined = jnp.concatenate([sent, received, edges_b], axis=1)
    return joined, dot(joined, w1_ref[...])


def edges_forward(
    b, count, table, nodes_ref, edges_ref, srow_ref, rrow_ref, w1_ref, w2_ref, g1_ref, inbound
):
    sent = send_gather(b, srow_ref, table)
    received = dot(receive_hits(b, rrow_ref), nodes_ref[tile_of(b), :]).astype(BF16)
    edges_b = edges_ref[block_of(b), :]
    joined, z = edge_hidden(sent, received, edges_b, w1_ref)
    hidden = (z * sigmoid(z)).astype(BF16)
    n, rstd = layer_norm(dot(hidden, w2_ref[...]))
    message = n * g1_ref[...] * live_of(b, count)
    edges_next = (edges_b.astype(F32) + message).astype(BF16)
    back = hits_t(flat_row(block_rows(rrow_ref, b), BLOCK // 128), TILE)
    inbound[tile_of(b), :] += dot(back, message.astype(BF16))
    return sent, joined, z, hidden, n, rstd, edges_next


def nodes_forward(nodes_b, inbound_b, u1_ref, u2_ref, g2_ref):
    joined = jnp.concatenate([nodes_b, inbound_b], axis=1)
    z = dot(joined, u1_ref[...])
    hidden = (z * sigmoid(z)).astype(BF16)
    n, rstd = layer_norm(dot(hidden, u2_ref[...]))
    nodes_next = (nodes_b.astype(F32) + n * g2_ref[...]).astype(BF16)
    return joined, z, hidden, n, rstd, nodes_next


def nodes_backward(grad, joined, z, hidden, n, rstd, u1_ref, u2_ref, g2_ref, sums):
    sums[897:898, :] = jnp.sum(grad * n, axis=0, keepdims=True)
    dy = layer_norm_grad(grad * g2_ref[...], n, rstd).astype(BF16)
    sums[768:896, :] = dot_tn(hidden, dy)
    dz = (dot_nt(dy, u2_ref[...]).astype(BF16).astype(F32) * silu_grad(z)).astype(BF16)
    sums[512:768, :] = dot_tn(joined, dz)
    back = dot_nt(dz, u1_ref[...]).astype(BF16)
    return back[:, :L].astype(F32), back[:, L:]


def edges_backward(
    b, count, joined, z, hidden, n, rstd, grad_ref, dinbound, srow_ref, rrow_ref, w1_ref, w2_ref,
    g1_ref, sums, dnodes, dtable
):
    grad = grad_ref[block_of(b), :].astype(F32)
    from_nodes = dot(receive_hits(b, rrow_ref), dinbound[tile_of(b), :])
    dmessage = (grad + from_nodes) * live_of(b, count)
    sums[896:897, :] += jnp.sum(dmessage * n, axis=0, keepdims=True)
    dy = layer_norm_grad(dmessage * g1_ref[...], n, rstd).astype(BF16)
    sums[384:512, :] += dot_tn(hidden, dy)
    dz = (dot_nt(dy, w2_ref[...]).astype(BF16).astype(F32) * silu_grad(z)).astype(BF16)
    sums[0:384, :] += dot_tn(joined, dz)
    back = dot_nt(dz, w1_ref[...]).astype(BF16)
    dsent, dreceived, dedges = (back[:, :L], back[:, L : 2 * L], back[:, 2 * L :])
    row = flat_row(block_rows(srow_ref, b), BLOCK // 128)
    col = column(block_rows(srow_ref, b), BLOCK // 128)
    upper = col >= float(HALF)
    zero = jnp.zeros_like(dsent)
    dsent32 = dsent.astype(F32)
    pair = jnp.concatenate(
        [jnp.where(upper, 0.0, dsent32).astype(BF16), jnp.where(upper, dsent32, 0.0).astype(BF16)],
        axis=1,
    )
    dtable[...] += dot(hits_t(jnp.where(row >= float(HALF), row - float(HALF), row), HALF), pair)
    back_hits = hits_t(flat_row(block_rows(rrow_ref, b), BLOCK // 128), TILE)
    dnodes[tile_of(b), :] += dot(back_hits, dreceived)
    return grad + dedges.astype(F32)


def pack(sums, out_ref):
    gains = sums[896:898, :]
    sums[898:900, :] = gains - gains.astype(BF16).astype(F32)
    out_ref[...] = sums[...].astype(BF16)


def ghost_grads(dtable, out_ref):
    out_ref[0 : HALF - NODES, :] = dtable[NODES:HALF, 0:L].astype(BF16)
    out_ref[HALF - NODES :, :] = dtable[:, L : 2 * L].astype(BF16)


def add_returned(partial, returned_ref, ghost_row_ref):
    row = flat_row(ghost_row_ref[...], SLOTS)
    return partial + dot(hits_t(row, NODES), returned_ref[...])


def pick_kernel(nodes_ref, ghost_row_ref, picked_ref):
    pick(nodes_ref[...], ghost_row_ref, picked_ref)


def first_kernel(
    count_ref, nodes_ref, ghosts_ref, edges_ref, srow_ref, rrow_ref, ghost_row_ref, w1_ref, w2_ref,
    g1_ref, u1_ref, u2_ref, g2_ref, nodes_out, edges_out, sent_out, inbound_out, picked_out, table,
    inbound
):
    count = count_ref[0, 0]
    build_table(nodes_ref, ghosts_ref, table)
    inbound[...] = jnp.zeros_like(inbound)

    def step(b, carry):
        sent, _, _, _, _, _, edges_next = edges_forward(
            b, count, table, nodes_ref, edges_ref, srow_ref, rrow_ref, w1_ref, w2_ref, g1_ref,
            inbound
        )
        sent_out[block_of(b), :] = sent
        edges_out[block_of(b), :] = edges_next
        return carry

    lax.fori_loop(0, BLOCKS, step, 0)
    inbound_b = inbound[...].astype(BF16)
    inbound_out[...] = inbound_b
    nodes_next = nodes_forward(nodes_ref[...], inbound_b, u1_ref, u2_ref, g2_ref)[-1]
    nodes_out[...] = nodes_next
    pick(nodes_next, ghost_row_ref, picked_out)


def middle_kernel(
    count_ref, nodes_ref, ghosts_ref, edges_ref, srow_ref, rrow_ref, w1_ref, w2_ref, g1_ref, u1_ref,
    u2_ref, g2_ref, node_grad_ref, edge_grad_ref, nodes_out, edges_out, ghost_grad_out,
    edge_grad_out, node_grad_out, packed_out, table, inbound, joined_all, z_all, hidden_all, n_all,
    rstd_all, dinbound, dtable, sums
):
    count = count_ref[0, 0]
    build_table(nodes_ref, ghosts_ref, table)
    inbound[...] = jnp.zeros_like(inbound)

    def forward_step(b, carry):
        _, joined, z, hidden, n, rstd, edges_next = edges_forward(
            b, count, table, nodes_ref, edges_ref, srow_ref, rrow_ref, w1_ref, w2_ref, g1_ref,
            inbound
        )
        edges_out[block_of(b), :] = edges_next
        joined_all[block_of(b), :] = joined
        z_all[block_of(b), :] = z
        hidden_all[block_of(b), :] = hidden
        n_all[block_of(b), :] = n
        rstd_all[block_of(b), :] = jnp.broadcast_to(rstd, (BLOCK, L))
        return carry

    lax.fori_loop(0, BLOCKS, forward_step, 0)
    nodes_b = nodes_ref[...]
    joined, z, hidden, n, rstd, nodes_next = nodes_forward(
        nodes_b, inbound[...].astype(BF16), u1_ref, u2_ref, g2_ref
    )
    nodes_out[...] = nodes_next
    node_grad = node_grad_ref[...].astype(F32)
    sums[...] = jnp.zeros_like(sums)
    through, dinbound[...] = nodes_backward(
        node_grad, joined, z, hidden, n, rstd, u1_ref, u2_ref, g2_ref, sums
    )
    node_grad_out[...] = node_grad + through
    dtable[...] = jnp.zeros_like(dtable)

    def backward_step(b, carry):
        at = block_of(b)
        edge_grad = edges_backward(
            b, count, joined_all[at, :], z_all[at, :], hidden_all[at, :], n_all[at, :],
            rstd_all[at, :], edge_grad_ref, dinbound, srow_ref, rrow_ref, w1_ref, w2_ref, g1_ref,
            sums, node_grad_out, dtable
        )
        edge_grad_out[at, :] = edge_grad.astype(BF16)
        return carry

    lax.fori_loop(0, BLOCKS, backward_step, 0)
    pack(sums, packed_out)
    ghost_grads(dtable, ghost_grad_out)
    node_grad_out[...] += dtable[0:NODES, 0:L]


def last_kernel(
    count_ref, nodes_ref, inbound_ref, sent_ref, edges_ref, srow_ref, rrow_ref, ghost_row_ref,
    w1_ref, w2_ref, g1_ref, u1_ref, u2_ref, g2_ref, partial_ref, returned_ref, edge_grad_ref,
    ghost_grad_out, edge_grad_out, node_grad_out, packed_out, dinbound, dtable, sums
):
    count = count_ref[0, 0]
    node_grad = add_returned(partial_ref[...], returned_ref, ghost_row_ref)
    node_grad = node_grad.astype(BF16).astype(F32)
    joined, z, hidden, n, rstd, _ = nodes_forward(
        nodes_ref[...], inbound_ref[...], u1_ref, u2_ref, g2_ref
    )
    sums[...] = jnp.zeros_like(sums)
    through, dinbound[...] = nodes_backward(
        node_grad, joined, z, hidden, n, rstd, u1_ref, u2_ref, g2_ref, sums
    )
    node_grad_out[...] = node_grad + through
    dtable[...] = jnp.zeros_like(dtable)

    def backward_step(b, carry):
        at = block_of(b)
        received = dot(receive_hits(b, rrow_ref), nodes_ref[tile_of(b), :]).astype(BF16)
        joined, z = edge_hidden(sent_ref[at, :], received, edges_ref[at, :], w1_ref)
        hidden = (z * sigmoid(z)).astype(BF16)
        n, rstd = layer_norm(dot(hidden, w2_ref[...]))
        edge_grad_out[at, :] = edges_backward(
            b, count, joined, z, hidden, n, rstd, edge_grad_ref, dinbound, srow_ref, rrow_ref,
            w1_ref, w2_ref, g1_ref, sums, node_grad_out, dtable
        )
        return carry

    lax.fori_loop(0, BLOCKS, backward_step, 0)
    pack(sums, packed_out)
    ghost_grads(dtable, ghost_grad_out)
    node_grad_out[...] += dtable[0:NODES, 0:L]


def return_kernel(partial_ref, returned_ref, ghost_row_ref, out_ref):
    out_ref[...] = add_returned(partial_ref[...], returned_ref, ghost_row_ref)


def call(kernel, outs, scratch, scalars, *args):
    vmem = pl.BlockSpec(memory_space=pltpu.VMEM)
    smem = pl.BlockSpec(memory_space=pltpu.SMEM)
    return pl.pallas_call(
        kernel,
        out_shape=[jax.ShapeDtypeStruct(s, d) for s, d in outs],
        in_specs=[smem] * scalars + [vmem] * (len(args) - scalars),
        out_specs=[vmem] * len(outs),
        scratch_shapes=[pltpu.VMEM(s, d) for s, d in scratch],
        compiler_params=pltpu.CompilerParams(vmem_limit_bytes=40 * 1024 * 1024),
    )(*args)


def exchange(slabs):
    up = [(i, i + 1) for i in range(lax.axis_size("gx") - 1)]
    down = [(j, i) for i, j in up]
    rows = slabs.reshape(SLOTS, G, L)
    low, high = (rows[0:3], rows[5:8])
    from_before = lax.ppermute(high, "gx", up)
    from_after = lax.ppermute(low, "gx", down)
    left = jnp.stack([from_before[0], rows[3], from_after[0]], axis=0)
    right = jnp.stack([from_before[2], rows[4], from_after[2]], axis=0)
    up = [(i, i + 1) for i in range(lax.axis_size("gy") - 1)]
    down = [(j, i) for i, j in up]
    before = lax.ppermute(right, "gy", up)
    after = lax.ppermute(left, "gy", down)
    return jnp.concatenate(
        [
            before[0], from_before[1], after[0], before[1], after[1], before[2], from_after[1],
            after[2],
        ],
        axis=0,
    )


def sum_over_domains(packed):
    axes = ("gx", "gy")
    devices = lax.axis_size(axes)
    parts = packed.reshape(devices, -1, L)
    parts = lax.all_to_all(parts, axes, 0, 0, tiled=True)
    mine = jnp.sum(parts.astype(F32), axis=0).astype(BF16)
    copies = jnp.broadcast_to(mine[None], parts.shape)
    whole = lax.all_to_all(copies, axes, 0, 0, tiled=True)
    return whole.reshape(LAYERS, PACKED, L).astype(F32)


def on_device(
    latents,
    edge_latents,
    senders,
    receivers,
    ghost_rows,
    edge_count,
    node_cotangent,
    edge_cotangent,
    edge_first,
    edge_second,
    edge_scale,
    node_first,
    node_second,
    node_scale,
):
    nodes0 = latents[0, 0]
    edges0 = edge_latents[0, 0]
    ids = senders[0, 0]
    srow = jnp.where(ids >= NODES + 4 * G, ids - G, ids).astype(F32).reshape(-1, 128)
    rrow = receivers[0, 0].astype(F32).reshape(-1, 128)
    slots = ghost_rows[0, 0].reshape(9, G)
    grow = jnp.concatenate([slots[:4], slots[5:]], axis=0).astype(F32)

    def weights(i):
        return (
            edge_first[i],
            edge_second[i],
            edge_scale[i : i + 1],
            node_first[i],
            node_second[i],
            node_scale[i : i + 1],
        )

    node_b = ((NODES, L), BF16)
    node_f = ((NODES, L), F32)
    edge_b = ((EDGES, L), BF16)
    edge_f = ((EDGES, L), F32)
    ghost_b = ((GHOSTS, L), BF16)
    packed = ((PACKED, L), BF16)
    packed_f = ((PACKED, L), F32)
    table_b = ((HALF, 2 * L), BF16)
    table_f = ((HALF, 2 * L), F32)

    (picked,) = call(pick_kernel, [ghost_b], [], 0, nodes0, grow)
    ghosts = exchange(picked)
    nodes1, edges1, sent, inbound, picked = call(
        first_kernel, [node_b, edge_b, edge_b, node_b, ghost_b], [table_b, node_f], 1,
        edge_count, nodes0, ghosts, edges0, srow, rrow, grow, *weights(0)
    )
    ghosts = exchange(picked)
    nodes2, edges2, ghost_grad, edge_grad, partial, packed1 = call(
        middle_kernel, [node_b, edge_b, ghost_b, edge_b, node_f, packed],
        [table_b, node_f, ((EDGES, 3 * L), BF16), edge_f, edge_b, edge_f, edge_f, node_b, table_f,
         packed_f],
        1, edge_count, nodes1, ghosts, edges1, srow, rrow, *weights(1), node_cotangent[0, 0],
        edge_cotangent[0, 0]
    )
    returned = exchange(ghost_grad)
    ghost_grad, edge_grad, partial, packed0 = call(
        last_kernel, [ghost_b, edge_f, node_f, packed], [node_b, table_f, packed_f], 1,
        edge_count, nodes0, inbound, sent, edges0, srow, rrow, grow, *weights(0), partial,
        returned, edge_grad
    )
    returned = exchange(ghost_grad)
    (node_grad,) = call(return_kernel, [node_f], [], 0, partial, returned, grow)
    total = sum_over_domains(jnp.concatenate([packed0, packed1], axis=0))
    return (
        nodes2[None, None],
        edges2[None, None],
        node_grad[None, None],
        edge_grad[None, None],
        total[:, 0:384],
        total[:, 384:512],
        total[:, 896] + total[:, 898],
        total[:, 512:768],
        total[:, 768:896],
        total[:, 897] + total[:, 899],
    )


def solution(mesh):
    domain = P("gx", "gy", None, None)
    placed = (
        domain,
        domain,
        P("gx", "gy", None),
        P("gx", "gy", None),
        P("gx", "gy", None, None, None),
        P("gx", "gy"),
        domain,
        domain,
        P(),
        P(),
        P(),
        P(),
        P(),
        P(),
    )
    return jax.shard_map(
        on_device,
        mesh=mesh,
        in_specs=placed,
        out_specs=(domain, domain, domain, domain, P(), P(), P(), P(), P(), P()),
        check_vma=False,
    )
```

time: 570 us -> 215 us (0.38); the launches traced: 561 us -> 214 us
  waiting for transfers between devices: 186 us -> 50.7 us
  other arithmetic: 122 us -> 4.13 us
  blocking collectives: 112 us -> 0 us
  Pallas kernels: 0 us -> 54.3 us
  starting transfers between devices: 43 us -> 95.5 us
  local copies, waits for them, and re-layouts: 48.1 us -> 7.86 us
  matrix products: 33.6 us -> 0 us
  between operations: 17 us -> 1.87 us
    psum x1 -> x0, waiting for transfers between devices: 171 us -> none  [on_device(): lax.psum((param_grad[0], param_grad[1], param_grad[2], param_grad[3], par...]
    psum x1 -> x0, blocking collectives: 112 us -> none  [on_device(): lax.psum((param_grad[0], param_grad[1], param_grad[2], param_grad[3], par...]
    scatter-add x4 -> x0, other arithmetic: 65.6 us -> none  [the longest x2 47.2 us: layer_update(): sender_rows = jnp.take(node_table, sender_ids, axis=0).astype(jnp.bfloat16)]
    pallas_call x0 -> x5, Pallas kernels: none -> 54.3 us  [call(): pl.pallas_call(kernel, out_shape=[jax.ShapeDtypeStruct(s, d) for s, d in...]
    all_to_all x0 -> x2, starting transfers between devices: none -> 49.1 us  [the longest x1 41.3 us: sum_over_domains(): parts = lax.all_to_all(parts, axes, 0, 0, tiled=True)]
    dot_general x33 -> x0, matrix products: 33.6 us -> none  [the longest x6 7.34 us: layer_update(): jnp.dot(joined, edge_first.astype(jnp.bfloat16), preferred_element_type=j...]
    gather x4 -> x0, local copies, waits for them, and re-layouts: 33.5 us -> none  [the longest x2 27.2 us: layer_update(): sender_rows = jnp.take(node_table, sender_ids, axis=0).astype(jnp.bfloat16)]
    all_to_all x0 -> x2, waiting for transfers between devices: none -> 30.3 us  [the longest x1 20 us: sum_over_domains(): whole = lax.all_to_all(copies, axes, 0, 0, tiled=True)]
  transfers between devices with their start and end apart: 17 -> 18, of which waited for: 6 -> 9; matrix products, arithmetic and copies ran while one was open for 5% -> 3% of each run, Pallas kernels for 0% -> 1%
where the time goes in v1:
time: 215 us; the launch traced here: 214 us
  starting transfers between devices  95.5 us (44%)
  Pallas kernels  54.3 us (25%)
  waiting for transfers between devices  50.7 us (24%)
  local copies, waits for them, and re-layouts  7.86 us (4%)
  other arithmetic  4.13 us (2%)
    pallas_call x5, Pallas kernels, call(): pl.pallas_call(kernel, out_shape=[jax.ShapeDtypeStruct(s, d) for s, d in...  54.3 us
    all_to_all x1, starting transfers between devices, sum_over_domains(): parts = lax.all_to_all(parts, axes, 0, 0, tiled=True)  41.3 us
    ppermute x4, starting transfers between devices, exchange(): from_before = lax.ppermute(high, 'gx', up)  20 us
    all_to_all x1, waiting for transfers between devices, sum_over_domains(): whole = lax.all_to_all(copies, axes, 0, 0, tiled=True)  20 us
    ppermute x4, waiting for transfers between devices, exchange(): after = lax.ppermute(left, 'gy', down)  17 us
    ppermute x4, starting transfers between devices, exchange(): before = lax.ppermute(right, 'gy', up)  13.5 us
    all_to_all x1, waiting for transfers between devices, sum_over_domains(): parts = lax.all_to_all(parts, axes, 0, 0, tiled=True)  10.3 us
    ppermute x4, starting transfers between devices, exchange(): after = lax.ppermute(left, 'gy', down)  7.83 us
  transfers between devices with their start and end apart: 18, of which 9 were waited for; matrix products, arithmetic and copies ran while one was open for 3% of the time, Pallas kernels for 1%

profile of v1, /device:TPU:1, one launch (start us, length us, event | category | flops | bytes accessed | tf_op | source)
XLA Modules:
  0.0 214.4 jit_solution(14789358877492044071)
XLA Ops:
  0.6 0.0 copy-start
  0.7 0.8 reduce.1
  1.5 0.0 copy-start.1
  1.5 0.9 copy-done.1
  2.4 0.5 shard_map.213
  2.9 1.3 collective-permute-start.1
  4.2 5.0 %collective-permute-start = (bf16[3,128,128]{2,1,0:T(8,128)(2,1)S(1)}, bf16[3,128,128]{2,1,0:T(8,128)(2,1)S(1)}, u32[]{:S(2)}, u32[]{:S(2)}) collective-permute-start(bf16[3,128,128]{2,1,0:T(8,128)(2,1)S(1)} %bitcast.198), channel_id=1, source_target_pairs={{0,16},{16,32},{32,48},{48,64},{64,80},{80,96},{96,112},{112,128},... | collective-permute-start | bytes 294920 | tf_op jit(solution)/shard_map/ppermute | solution.py:356
  9.2 0.7 fusion.srow_ref
  10.0 0.9 slice_bitcast_fusion.2
  10.8 1.0 slice_bitcast_fusion
  11.8 0.8 slice_bitcast_fusion.42
  12.6 0.8 fusion.15
  14.1 0.7 convert_element_type.24
  14.8 0.0 collective-permute-done.1
  14.8 0.0 collective-permute-done
  14.9 4.1 %collective-permute-start.2 = (bf16[3,128,128]{2,1,0:T(8,128)(2,1)S(1)}, bf16[3,128,128]{2,1,0:T(8,128)(2,1)S(1)}, u32[]{:S(2)}, u32[]{:S(2)}) collective-permute-start(bf16[3,128,128]{2,1,0:T(8,128)(2,1)S(1)} %pad_maximum_fusion), channel_id=1, source_target_pairs={{0,1},{1,2},{2,3},{3,4},{4,5},{5,6},{6,7},{7,8},{8,9},{9,10},{10,1... | collective-permute-start | bytes 294920 | tf_op jit(solution)/shard_map/ppermute | solution.py:362
  18.9 0.0 copy-start.3
  18.9 0.0 copy-start.4
  19.0 2.1 collective-permute-start.3
  21.0 0.0 collective-permute-done.2
  21.1 4.0 %collective-permute-done.3 = bf16[3,128,128]{2,1,0:T(8,128)(2,1)S(1)} collective-permute-done((bf16[3,128,128]{2,1,0:T(8,128)(2,1)S(1)}, bf16[3,128,128]{2,1,0:T(8,128)(2,1)S(1)}, u32[]{:S(2)}, u32[]{:S(2)}) %collective-permute-start.3) | collective-permute-done | bytes 98336 | tf_op jit(solution)/shard_map/ppermute | solution.py:363
  25.1 0.0 copy-done
  25.1 11.7 %shard_map.214 = (bf16[512,128]{1,0:T(8,128)(2,1)S(1)}, bf16[4096,128]{1,0:T(8,128)(2,1)S(1)}, bf16[4096,128]{1,0:T(8,128)(2,1)S(1)}, bf16[512,128]{1,0:T(8,128)(2,1)S(1)}, bf16[1024,128]{1,0:T(8,128)(2,1)S(1)}) custom-call(s32[1,1]{1,0:T(1,128)S(6)} %copy.57.count_ref, bf16[512,128]{1,0:T(8,128)(2,1)S(1)} %bitcast.189, ...), custom_call_target="tpu_custom_call" | custom-call | tf_op jit(solution)/shard_map/pallas_call | solution.py:341
  36.9 1.3 collective-permute-start.5
  38.2 4.2 %collective-permute-start.4 = (bf16[3,128,128]{2,1,0:T(8,128)(2,1)S(1)}, bf16[3,128,128]{2,1,0:T(8,128)(2,1)S(1)}, u32[]{:S(2)}, u32[]{:S(2)}) collective-permute-start(bf16[3,128,128]{2,1,0:T(8,128)(2,1)S(1)} %bitcast.201), channel_id=1, source_target_pairs={{0,16},{16,32},{32,48},{48,64},{64,80},{80,96},{96,112},{112,128},... | collective-permute-start | bytes 294920 | tf_op jit(solution)/shard_map/ppermute | solution.py:356
  42.4 0.0 collective-permute-done.5
  42.4 1.6 collective-permute-done.4
  44.0 3.2 %collective-permute-start.6 = (bf16[3,128,128]{2,1,0:T(8,128)(2,1)S(1)}, bf16[3,128,128]{2,1,0:T(8,128)(2,1)S(1)}, u32[]{:S(2)}, u32[]{:S(2)}) collective-permute-start(bf16[3,128,128]{2,1,0:T(8,128)(2,1)S(1)} %pad_maximum_fusion.2), channel_id=1, source_target_pairs={{0,1},{1,2},{2,3},{3,4},{4,5},{5,6},{6,7},{7,8},{8,9},{9,10},{10,1... | collective-permute-start | bytes 294920 | tf_op jit(solution)/shard_map/ppermute | solution.py:362
  47.2 1.9 collective-permute-start.7
  49.2 0.0 collective-permute-done.6
  49.2 4.0 %collective-permute-done.7 = bf16[3,128,128]{2,1,0:T(8,128)(2,1)S(1)} collective-permute-done((bf16[3,128,128]{2,1,0:T(8,128)(2,1)S(1)}, bf16[3,128,128]{2,1,0:T(8,128)(2,1)S(1)}, u32[]{:S(2)}, u32[]{:S(2)}) %collective-permute-start.7) | collective-permute-done | bytes 98336 | tf_op jit(solution)/shard_map/ppermute | solution.py:363
  53.2 0.0 copy-done.3
  53.3 0.0 copy-start.2
  53.3 22.8 %shard_map.215 = (bf16[512,128]{1,0:T(8,128)(2,1)}, bf16[4096,128]{1,0:T(8,128)(2,1)}, bf16[1024,128]{1,0:T(8,128)(2,1)S(1)}, bf16[4096,128]{1,0:T(8,128)(2,1)S(...) custom-call(s32[1,1]{1,0:T(1,128)S(6)} %copy.57.count_ref, bf16[512,128]{1,0:T(8,128)(2,1)S(1)} %get-tuple-element.25.nodes_ref, ...), custom_call_target="tpu_custom_call" | custom-call | tf_op jit(solution)/shard_map/pallas_call | solution.py:341
  76.1 1.3 collective-permute-start.9
  77.4 4.7 %collective-permute-start.8 = (bf16[3,128,128]{2,1,0:T(8,128)(2,1)S(1)}, bf16[3,128,128]{2,1,0:T(8,128)(2,1)S(1)}, u32[]{:S(2)}, u32[]{:S(2)}) collective-permute-start(bf16[3,128,128]{2,1,0:T(8,128)(2,1)S(1)} %bitcast.202), channel_id=1, source_target_pairs={{0,16},{16,32},{32,48},{48,64},{64,80},{80,96},{96,112},{112,128},... | collective-permute-start | bytes 294920 | tf_op jit(solution)/shard_map/ppermute | solution.py:356
  82.1 0.0 collective-permute-done.9
  82.2 1.6 collective-permute-done.8
  83.8 2.7 %collective-permute-start.10 = (bf16[3,128,128]{2,1,0:T(8,128)(2,1)S(1)}, bf16[3,128,128]{2,1,0:T(8,128)(2,1)S(1)}, u32[]{:S(2)}, u32[]{:S(2)}) collective-permute-start(bf16[3,128,128]{2,1,0:T(8,128)(2,1)S(1)} %pad_maximum_fusion.4), channel_id=1, source_target_pairs={{0,1},{1,2},{2,3},{3,4},{4,5},{5,6},{6,7},{7,8},{8,9},{9,10},{10,1... | collective-permute-start | bytes 294920 | tf_op jit(solution)/shard_map/ppermute | solution.py:362
  86.5 1.9 collective-permute-start.11
  88.4 0.0 collective-permute-done.10
  88.5 4.0 %collective-permute-done.11 = bf16[3,128,128]{2,1,0:T(8,128)(2,1)S(1)} collective-permute-done((bf16[3,128,128]{2,1,0:T(8,128)(2,1)S(1)}, bf16[3,128,128]{2,1,0:T(8,128)(2,1)S(1)}, u32[]{:S(2)}, u32[]{:S(2)}) %collective-permute-start.11) | collective-permute-done | bytes 98336 | tf_op jit(solution)/shard_map/ppermute | solution.py:363
  92.5 18.2 %shard_map.216 = (bf16[1024,128]{1,0:T(8,128)(2,1)S(1)}, f32[4096,128]{1,0:T(8,128)}, f32[512,128]{1,0:T(8,128)S(1)}, bf16[1024,128]{1,0:T(8,128)(2,1)S(1)}) custom-call(s32[1,1]{1,0:T(1,128)S(6)} %copy.57.count_ref, bf16[512,128]{1,0:T(8,128)(2,1)S(1)} %bitcast.190, bf16[512,128]{1,0:T(8,128)(2,1)S(1)} %get-tuple-element.30.inbound_ref, ...), custom_call_target="tpu_custom_call" | custom-call | tf_op jit(solution)/shard_map/pallas_call | solution.py:341
  110.7 1.3 collective-permute-start.13
  112.0 6.0 %collective-permute-start.12 = (bf16[3,128,128]{2,1,0:T(8,128)(2,1)S(1)}, bf16[3,128,128]{2,1,0:T(8,128)(2,1)S(1)}, u32[]{:S(2)}, u32[]{:S(2)}) collective-permute-start(bf16[3,128,128]{2,1,0:T(8,128)(2,1)S(1)} %bitcast.200), channel_id=1, source_target_pairs={{0,16},{16,32},{32,48},{48,64},{64,80},{80,96},{96,112},{112,128},... | collective-permute-start | bytes 294920 | tf_op jit(solution)/shard_map/ppermute | solution.py:356
  118.1 0.8 maximum_bitcast_fusion
  118.9 41.3 %all-to-all-start = ((bf16[256,8,128]{2,1,0:T(8,128)(2,1)}), bf16[256,8,128]{2,1,0:T(8,128)(2,1)S(1)}, u32[]{:S(2)}, u32[]{:S(2)}) async-start(bf16[256,8,128]{2,1,0:T(8,128)(2,1)} %maximum_bitcast_fusion), calls=%async_computation | async-start | bytes 1048576 | tf_op jit(solution)/shard_map/all_to_all | solution.py:377
  160.2 0.0 collective-permute-done.13
  160.2 0.0 collective-permute-done.12
  160.3 3.5 %collective-permute-start.14 = (bf16[3,128,128]{2,1,0:T(8,128)(2,1)S(1)}, bf16[3,128,128]{2,1,0:T(8,128)(2,1)S(1)}, u32[]{:S(2)}, u32[]{:S(2)}) collective-permute-start(bf16[3,128,128]{2,1,0:T(8,128)(2,1)S(1)} %pad_maximum_fusion.6), channel_id=1, source_target_pairs={{0,1},{1,2},{2,3},{3,4},{4,5},{5,6},{6,7},{7,8},{8,9},{9,10},{10,1... | collective-permute-start | bytes 294920 | tf_op jit(solution)/shard_map/ppermute | solution.py:362
  163.9 1.9 collective-permute-start.15
  165.8 0.2 collective-permute-done.14
  166.0 5.1 %collective-permute-done.15 = bf16[3,128,128]{2,1,0:T(8,128)(2,1)S(1)} collective-permute-done((bf16[3,128,128]{2,1,0:T(8,128)(2,1)S(1)}, bf16[3,128,128]{2,1,0:T(8,128)(2,1)S(1)}, u32[]{:S(2)}, u32[]{:S(2)}) %collective-permute-start.15) | collective-permute-done | bytes 98336 | tf_op jit(solution)/shard_map/ppermute | solution.py:363
  171.1 10.3 %all-to-all-done = bf16[256,8,128]{2,1,0:T(8,128)(2,1)S(1)} async-done(((bf16[256,8,128]{2,1,0:T(8,128)(2,1)}), bf16[256,8,128]{2,1,0:T(8,128)(2,1)S(1)}, u32[]{:S(2)}, u32[]{:S(2)}) %all-to-all-start) | async-done | bytes 524320 | tf_op jit(solution)/shard_map/all_to_all | solution.py:377
  181.4 0.3 reduce_sum.12
  181.7 0.9 broadcast_in_dim.22
  182.5 7.8 %all-to-all-start.1 = ((bf16[256,8,128]{2,1,0:T(8,128)(2,1)}), bf16[256,8,128]{2,1,0:T(8,128)(2,1)S(1)}, u32[]{:S(2)}, u32[]{:S(2)}) async-start(bf16[256,8,128]{2,1,0:T(8,128)(2,1)} %broadcast_in_dim.22), calls=%async_computation.1 | async-start | bytes 1048576 | tf_op jit(solution)/shard_map/all_to_all | solution.py:380
  190.4 1.1 shard_map.217
  191.5 20.0 %all-to-all-done.1 = bf16[256,8,128]{2,1,0:T(8,128)(2,1)S(1)} async-done(((bf16[256,8,128]{2,1,0:T(8,128)(2,1)}), bf16[256,8,128]{2,1,0:T(8,128)(2,1)S(1)}, u32[]{:S(2)}, u32[]{:S(2)}) %all-to-all-start.1) | async-done | bytes 524320 | tf_op jit(solution)/shard_map/all_to_all | solution.py:380
  211.5 0.1 bitcast_convert_fusion
  211.6 0.6 slice_add_fusion
  212.1 0.7 slice.472
  212.9 0.7 fusion.1
  213.6 0.8 slice.468
  (61 shorter events, 0.6 us)
Async XLA Ops:
  0.6 24.5 %copy-start = (bf16[1,1,4096,128]{3,2,1,0:T(8,128)(2,1)S(1)}, bf16[1,1,4096,128]{3,2,1,0:T(8,128)(2,1)}, u32[]{:S(2)}) copy-start(bf16[1,1,4096,128]{3,2,1,0:T(8,128)(2,1)} %param.15) | copy-start | bytes 3145732
  1.5 0.9 copy-start.1
  2.9 11.9 %collective-permute-start.1 = (bf16[3,128,128]{2,1,0:T(8,128)(2,1)S(1)}, bf16[3,128,128]{2,1,0:T(8,128)(2,1)S(1)}, u32[]{:S(2)}, u32[]{:S(2)}) collective-permute-start(bf16[3,128,128]{2,1,0:T(8,128)(2,1)S(1)} %bitcast.199), channel_id=1, source_target_pairs={{16,0},{32,16},{48,32},{64,48},{80,64},{96,80},{112,96},{128,112},... | collective-permute-start | bytes 294920 | tf_op jit(solution)/shard_map/ppermute | solution.py:357
  4.2 10.6 %collective-permute-start = (bf16[3,128,128]{2,1,0:T(8,128)(2,1)S(1)}, bf16[3,128,128]{2,1,0:T(8,128)(2,1)S(1)}, u32[]{:S(2)}, u32[]{:S(2)}) collective-permute-start(bf16[3,128,128]{2,1,0:T(8,128)(2,1)S(1)} %bitcast.198), channel_id=1, source_target_pairs={{0,16},{16,32},{32,48},{48,64},{64,80},{80,96},{96,112},{112,128},... | collective-permute-start | bytes 294920 | tf_op jit(solution)/shard_map/ppermute | solution.py:356
  14.9 6.2 %collective-permute-start.2 = (bf16[3,128,128]{2,1,0:T(8,128)(2,1)S(1)}, bf16[3,128,128]{2,1,0:T(8,128)(2,1)S(1)}, u32[]{:S(2)}, u32[]{:S(2)}) collective-permute-start(bf16[3,128,128]{2,1,0:T(8,128)(2,1)S(1)} %pad_maximum_fusion), channel_id=1, source_target_pairs={{0,1},{1,2},{2,3},{3,4},{4,5},{5,6},{6,7},{7,8},{8,9},{9,10},{10,1... | collective-permute-start | bytes 294920 | tf_op jit(solution)/shard_map/ppermute | solution.py:362
  18.9 34.3 %copy-start.3 = (bf16[1,1,4096,128]{3,2,1,0:T(8,128)(2,1)S(1)}, bf16[1,1,4096,128]{3,2,1,0:T(8,128)(2,1)}, u32[]{:S(2)}) copy-start(bf16[1,1,4096,128]{3,2,1,0:T(8,128)(2,1)} %param.21) | copy-start | bytes 3145732
  18.9 34.3 %copy-start.4 = (bf16[1,1,512,128]{3,2,1,0:T(8,128)(2,1)S(1)}, bf16[1,1,512,128]{3,2,1,0:T(8,128)(2,1)}, u32[]{:S(2)}) copy-start(bf16[1,1,512,128]{3,2,1,0:T(8,128)(2,1)} %param.20) | copy-start | bytes 393220
  19.0 6.1 %collective-permute-start.3 = (bf16[3,128,128]{2,1,0:T(8,128)(2,1)S(1)}, bf16[3,128,128]{2,1,0:T(8,128)(2,1)S(1)}, u32[]{:S(2)}, u32[]{:S(2)}) collective-permute-start(bf16[3,128,128]{2,1,0:T(8,128)(2,1)S(1)} %pad_maximum_fusion.1), channel_id=1, source_target_pairs={{1,0},{2,1},{3,2},{4,3},{5,4},{6,5},{7,6},{8,7},{9,8},{10,9},{11,1... | collective-permute-start | bytes 294920 | tf_op jit(solution)/shard_map/ppermute | solution.py:363
  36.9 5.5 %collective-permute-start.5 = (bf16[3,128,128]{2,1,0:T(8,128)(2,1)S(1)}, bf16[3,128,128]{2,1,0:T(8,128)(2,1)S(1)}, u32[]{:S(2)}, u32[]{:S(2)}) collective-permute-start(bf16[3,128,128]{2,1,0:T(8,128)(2,1)S(1)} %bitcast.204), channel_id=1, source_target_pairs={{16,0},{32,16},{48,32},{64,48},{80,64},{96,80},{112,96},{128,112},... | collective-permute-start | bytes 294920 | tf_op jit(solution)/shard_map/ppermute | solution.py:357
  38.2 5.8 %collective-permute-start.4 = (bf16[3,128,128]{2,1,0:T(8,128)(2,1)S(1)}, bf16[3,128,128]{2,1,0:T(8,128)(2,1)S(1)}, u32[]{:S(2)}, u32[]{:S(2)}) collective-permute-start(bf16[3,128,128]{2,1,0:T(8,128)(2,1)S(1)} %bitcast.201), channel_id=1, source_target_pairs={{0,16},{16,32},{32,48},{48,64},{64,80},{80,96},{96,112},{112,128},... | collective-permute-start | bytes 294920 | tf_op jit(solution)/shard_map/ppermute | solution.py:356
  44.0 5.1 %collective-permute-start.6 = (bf16[3,128,128]{2,1,0:T(8,128)(2,1)S(1)}, bf16[3,128,128]{2,1,0:T(8,128)(2,1)S(1)}, u32[]{:S(2)}, u32[]{:S(2)}) collective-permute-start(bf16[3,128,128]{2,1,0:T(8,128)(2,1)S(1)} %pad_maximum_fusion.2), channel_id=1, source_target_pairs={{0,1},{1,2},{2,3},{3,4},{4,5},{5,6},{6,7},{7,8},{8,9},{9,10},{10,1... | collective-permute-start | bytes 294920 | tf_op jit(solution)/shard_map/ppermute | solution.py:362
  47.2 5.9 %collective-permute-start.7 = (bf16[3,128,128]{2,1,0:T(8,128)(2,1)S(1)}, bf16[3,128,128]{2,1,0:T(8,128)(2,1)S(1)}, u32[]{:S(2)}, u32[]{:S(2)}) collective-permute-start(bf16[3,128,128]{2,1,0:T(8,128)(2,1)S(1)} %pad_maximum_fusion.3), channel_id=1, source_target_pairs={{1,0},{2,1},{3,2},{4,3},{5,4},{6,5},{7,6},{8,7},{9,8},{10,9},{11,1... | collective-permute-start | bytes 294920 | tf_op jit(solution)/shard_map/ppermute | solution.py:363
  53.3 39.3 %copy-start.2 = (bf16[1,1,512,128]{3,2,1,0:T(8,128)(2,1)S(1)}, bf16[1,1,512,128]{3,2,1,0:T(8,128)(2,1)}, u32[]{:S(2)}) copy-start(bf16[1,1,512,128]{3,2,1,0:T(8,128)(2,1)} %param.14) | copy-start | bytes 393220
  76.1 6.1 %collective-permute-start.9 = (bf16[3,128,128]{2,1,0:T(8,128)(2,1)S(1)}, bf16[3,128,128]{2,1,0:T(8,128)(2,1)S(1)}, u32[]{:S(2)}, u32[]{:S(2)}) collective-permute-start(bf16[3,128,128]{2,1,0:T(8,128)(2,1)S(1)} %bitcast.205), channel_id=1, source_target_pairs={{16,0},{32,16},{48,32},{64,48},{80,64},{96,80},{112,96},{128,112},... | collective-permute-start | bytes 294920 | tf_op jit(solution)/shard_map/ppermute | solution.py:357
  77.4 6.4 %collective-permute-start.8 = (bf16[3,128,128]{2,1,0:T(8,128)(2,1)S(1)}, bf16[3,128,128]{2,1,0:T(8,128)(2,1)S(1)}, u32[]{:S(2)}, u32[]{:S(2)}) collective-permute-start(bf16[3,128,128]{2,1,0:T(8,128)(2,1)S(1)} %bitcast.202), channel_id=1, source_target_pairs={{0,16},{16,32},{32,48},{48,64},{64,80},{80,96},{96,112},{112,128},... | collective-permute-start | bytes 294920 | tf_op jit(solution)/shard_map/ppermute | solution.py:356
  83.8 4.7 %collective-permute-start.10 = (bf16[3,128,128]{2,1,0:T(8,128)(2,1)S(1)}, bf16[3,128,128]{2,1,0:T(8,128)(2,1)S(1)}, u32[]{:S(2)}, u32[]{:S(2)}) collective-permute-start(bf16[3,128,128]{2,1,0:T(8,128)(2,1)S(1)} %pad_maximum_fusion.4), channel_id=1, source_target_pairs={{0,1},{1,2},{2,3},{3,4},{4,5},{5,6},{6,7},{7,8},{8,9},{9,10},{10,1... | collective-permute-start | bytes 294920 | tf_op jit(solution)/shard_map/ppermute | solution.py:362
  86.5 5.9 %collective-permute-start.11 = (bf16[3,128,128]{2,1,0:T(8,128)(2,1)S(1)}, bf16[3,128,128]{2,1,0:T(8,128)(2,1)S(1)}, u32[]{:S(2)}, u32[]{:S(2)}) collective-permute-start(bf16[3,128,128]{2,1,0:T(8,128)(2,1)S(1)} %pad_maximum_fusion.5), channel_id=1, source_target_pairs={{1,0},{2,1},{3,2},{4,3},{5,4},{6,5},{7,6},{8,7},{9,8},{10,9},{11,1... | collective-permute-start | bytes 294920 | tf_op jit(solution)/shard_map/ppermute | solution.py:363
  110.7 49.5 %collective-permute-start.13 = (bf16[3,128,128]{2,1,0:T(8,128)(2,1)S(1)}, bf16[3,128,128]{2,1,0:T(8,128)(2,1)S(1)}, u32[]{:S(2)}, u32[]{:S(2)}) collective-permute-start(bf16[3,128,128]{2,1,0:T(8,128)(2,1)S(1)} %bitcast.203), channel_id=1, source_target_pairs={{16,0},{32,16},{48,32},{64,48},{80,64},{96,80},{112,96},{128,112},... | collective-permute-start | bytes 294920 | tf_op jit(solution)/shard_map/ppermute | solution.py:357
  112.0 48.2 %collective-permute-start.12 = (bf16[3,128,128]{2,1,0:T(8,128)(2,1)S(1)}, bf16[3,128,128]{2,1,0:T(8,128)(2,1)S(1)}, u32[]{:S(2)}, u32[]{:S(2)}) collective-permute-start(bf16[3,128,128]{2,1,0:T(8,128)(2,1)S(1)} %bitcast.200), channel_id=1, source_target_pairs={{0,16},{16,32},{32,48},{48,64},{64,80},{80,96},{96,112},{112,128},... | collective-permute-start | bytes 294920 | tf_op jit(solution)/shard_map/ppermute | solution.py:356
  118.9 62.5 %all-to-all-start = ((bf16[256,8,128]{2,1,0:T(8,128)(2,1)}), bf16[256,8,128]{2,1,0:T(8,128)(2,1)S(1)}, u32[]{:S(2)}, u32[]{:S(2)}) async-start(bf16[256,8,128]{2,1,0:T(8,128)(2,1)} %maximum_bitcast_fusion), calls=%async_computation | async-start | bytes 1048576 | tf_op jit(solution)/shard_map/all_to_all | solution.py:377
  160.3 5.7 %collective-permute-start.14 = (bf16[3,128,128]{2,1,0:T(8,128)(2,1)S(1)}, bf16[3,128,128]{2,1,0:T(8,128)(2,1)S(1)}, u32[]{:S(2)}, u32[]{:S(2)}) collective-permute-start(bf16[3,128,128]{2,1,0:T(8,128)(2,1)S(1)} %pad_maximum_fusion.6), channel_id=1, source_target_pairs={{0,1},{1,2},{2,3},{3,4},{4,5},{5,6},{6,7},{7,8},{8,9},{9,10},{10,1... | collective-permute-start | bytes 294920 | tf_op jit(solution)/shard_map/ppermute | solution.py:362
  163.9 7.2 %collective-permute-start.15 = (bf16[3,128,128]{2,1,0:T(8,128)(2,1)S(1)}, bf16[3,128,128]{2,1,0:T(8,128)(2,1)S(1)}, u32[]{:S(2)}, u32[]{:S(2)}) collective-permute-start(bf16[3,128,128]{2,1,0:T(8,128)(2,1)S(1)} %pad_maximum_fusion.7), channel_id=1, source_target_pairs={{1,0},{2,1},{3,2},{4,3},{5,4},{6,5},{7,6},{8,7},{9,8},{10,9},{11,1... | collective-permute-start | bytes 294920 | tf_op jit(solution)/shard_map/ppermute | solution.py:363
  182.5 29.0 %all-to-all-start.1 = ((bf16[256,8,128]{2,1,0:T(8,128)(2,1)}), bf16[256,8,128]{2,1,0:T(8,128)(2,1)S(1)}, u32[]{:S(2)}, u32[]{:S(2)}) async-start(bf16[256,8,128]{2,1,0:T(8,128)(2,1)} %broadcast_in_dim.22), calls=%async_computation.1 | async-start | bytes 1048576 | tf_op jit(solution)/shard_map/all_to_all | solution.py:380

commit v2 on v1

v2 whole, which is shorter than its diff:
```python
import functools

import jax
import jax.numpy as jnp
from jax import lax
from jax.experimental import pallas as pl
from jax.experimental.pallas import tpu as pltpu
from jax.sharding import PartitionSpec as P

L = 128
LAYERS = 2
TILE = 256
DEG = 8
G = 128
NODES = 512
EDGES = 4096
PART = TILE * DEG
BLOCK = 1024
BLOCKS = EDGES // BLOCK
PART_BLOCKS = PART // BLOCK
PACKED = 1024
OUTER = ((0, 0), (0, 1), (0, 2), (1, 0), (1, 2), (2, 0), (2, 1), (2, 2))

F32 = jnp.float32
BF16 = jnp.bfloat16
epsilon = 1e-05


def dot(a, b):
    return jnp.dot(a, b, preferred_element_type=F32)


def dot_nt(a, b):
    return lax.dot_general(a, b, (((1,), (1,)), ((), ())), preferred_element_type=F32)


def dot_tn(a, b):
    return lax.dot_general(a, b, (((0,), (0,)), ((), ())), preferred_element_type=F32)


def sigmoid(v):
    return 0.5 * jnp.tanh(0.5 * v) + 0.5


def column(row):
    parts = [
        jnp.transpose(jnp.broadcast_to(row[:, i : i + 128], (128, 128)))
        for i in range(0, row.shape[1], 128)
    ]
    return jnp.concatenate(parts, axis=0) if len(parts) > 1 else parts[0]


def hits(col, width):
    lane = lax.broadcasted_iota(jnp.int32, col.shape, 1)
    parts = [
        jnp.where(col == lane + 128 * t, 1.0, 0.0).astype(BF16) for t in range(width // 128)
    ]
    return jnp.concatenate(parts, axis=1)


def hits_t(row, height):
    sub = lax.broadcasted_iota(jnp.int32, (height, row.shape[1]), 0)
    return jnp.where(sub == row, 1.0, 0.0).astype(BF16)


def layer_norm(y):
    center = y - jnp.mean(y, axis=-1, keepdims=True)
    spread = jnp.mean(center * center, axis=-1, keepdims=True)
    rstd = lax.rsqrt(spread + epsilon)
    return center * rstd, rstd


def layer_norm_grad(dn, n, rstd):
    return rstd * (
        dn
        - jnp.mean(dn, axis=-1, keepdims=True)
        - n * jnp.mean(dn * n, axis=-1, keepdims=True)
    )


def silu_grad(z):
    s = sigmoid(z)
    return s * (1.0 + z * (1.0 - s))


def block_at(b):
    return pl.ds(pl.multiple_of(b * BLOCK, BLOCK), BLOCK)


def tile_at(b):
    return pl.ds(pl.multiple_of((b // PART_BLOCKS) * TILE, TILE), TILE)


def index_row(ref, b):
    return ref[:, block_at(b)]


def local_index(ids):
    return jnp.where(ids < TILE, ids, jnp.where(ids < NODES, ids - TILE, -1))


def ghost_index(ids):
    g = ids - NODES
    g = jnp.where(g >= 4 * G, g - G, g)
    return jnp.where(g >= NODES, g - NODES, g)


def ghost_upper(ids):
    return ids >= NODES + NODES + G


def live_of(b, count):
    slot = lax.broadcasted_iota(jnp.int32, (BLOCK, L), 0) + b * BLOCK
    return jnp.where(slot < count, 1.0, 0.0)


def pick(nodes_b, ghost_row_ref, slabs):
    for s, (i, j) in enumerate(OUTER):
        col = column(ghost_row_ref[i, j : j + 1, :])
        put_slab(slabs, s, dot(hits(col, NODES), nodes_b).astype(BF16))


def put_slab(slabs, s, value):
    low, same, high = slabs
    ref, i = ((low, s), (same, s - 3), (high, s - 5))[(s >= 3) + (s >= 5)]
    ref[i] = value


def arrived(refs):
    before, from_before, after, from_after = refs
    return [
        before[0], from_before[1], after[0], before[1], after[1], before[2], from_after[1], after[2]
    ]


def local_pair(nodes_ref):
    return jnp.concatenate([nodes_ref[0:TILE, :], nodes_ref[TILE:NODES, :]], axis=1)


def ghost_pair(ghost_refs):
    rows = arrived(ghost_refs)
    lower = jnp.concatenate(rows[:4], axis=0)
    upper = jnp.concatenate(rows[4:], axis=0)
    return jnp.concatenate([lower, upper], axis=1)


def nodes_forward(nodes_b, inbound_b, u1, u2, gain):
    joined = jnp.concatenate([nodes_b, inbound_b], axis=1)
    z = dot(joined, u1)
    hidden = (z * sigmoid(z)).astype(BF16)
    n, rstd = layer_norm(dot(hidden, u2))
    nodes_next = (nodes_b.astype(F32) + n * gain).astype(BF16)
    return joined, z, hidden, n, rstd, nodes_next


def nodes_backward(grad, joined, z, hidden, n, rstd, u1, u2, gain, sums):
    sums[384:512, :] = dot_tn(hidden, (dy := layer_norm_grad(grad * gain, n, rstd).astype(BF16)))
    sums[513:514, :] = jnp.sum(grad * n, axis=0, keepdims=True)
    dz = (dot_nt(dy, u2).astype(BF16).astype(F32) * silu_grad(z)).astype(BF16)
    sums[128:384, :] = dot_tn(joined, dz)
    back = dot_nt(dz, u1).astype(BF16)
    return back[:, :L].astype(F32), back[:, L:]


def before_kernel(part, layer, nodes_ref, edges_ref, send_ref, recv_ref, w1_ref, sent_out,
                  received_out, z_out):
    pair = local_pair(nodes_ref)
    tile = nodes_ref[part * TILE : (part + 1) * TILE, :]
    w1 = w1_ref[layer]

    def step(i, carry):
        b = i + part * PART_BLOCKS
        ids = index_row(send_ref, b)
        both = dot(hits(column(local_index(ids)), TILE), pair)
        sent = jnp.where(column(ids) >= TILE, both[:, L:], both[:, :L]).astype(BF16)
        received = dot(hits(column(index_row(recv_ref, b)), TILE), tile).astype(BF16)
        sent_out[block_at(i), :] = sent
        received_out[block_at(i), :] = received
        joined = jnp.concatenate([sent, received, edges_ref[block_at(b), :]], axis=1)
        z_out[block_at(i), :] = dot(joined, w1)
        return carry

    lax.fori_loop(0, PART_BLOCKS, step, 0, unroll=True)


def edges_forward(b, local, count, table, edges_ref, send_ref, recv_ref, w1s, w2, gain, inbound,
                  edges_out, sent_out, z_out, n_out, rstd_out):
    sent_ref, z_ref, i = local
    ids = index_row(send_ref, b)
    both = dot(hits(column(ghost_index(ids)), NODES), table)
    sent = jnp.where(column(ids) >= 2 * NODES + G, both[:, L:], both[:, :L]).astype(BF16)
    z = z_ref[block_at(i), :] + dot(sent, w1s)
    hidden = (z * sigmoid(z)).astype(BF16)
    n, rstd = layer_norm(dot(hidden, w2))
    message = n * gain * live_of(b, count)
    at = block_at(b)
    edges_out[at, :] = (edges_ref[at, :].astype(F32) + message).astype(BF16)
    inbound[tile_at(b), :] += dot(hits_t(index_row(recv_ref, b), TILE), message.astype(BF16))
    sent_out[at, :] = sent_ref[block_at(i), :] + sent
    z_out[at, :] = z
    n_out[at, :] = n
    rstd_out[at, :] = jnp.broadcast_to(rstd, (BLOCK, L))


def all_edges_forward(count, locals_, ghost_refs, table, edges_ref, send_ref, recv_ref, w1s, w2,
                      gain, inbound, outs):
    table[...] = ghost_pair(ghost_refs)
    inbound[...] = jnp.zeros_like(inbound)
    for part in range(2):
        sent_ref, z_ref = locals_[2 * part : 2 * part + 2]

        def step(i, carry, part=part, sent_ref=sent_ref, z_ref=z_ref):
            edges_forward(
                i + part * PART_BLOCKS, (sent_ref, z_ref, i), count, table[...], edges_ref,
                send_ref, recv_ref, w1s, w2, gain, inbound, *outs
            )
            return carry

        lax.fori_loop(0, PART_BLOCKS, step, 0, unroll=True)


def edges_backward(b, count, grad_ref, dinbound, z_ref, n_ref, rstd_ref, send_ref, recv_ref, w1s,
                   w2, gain, dy_out, dz_out, dsent_out, gain_sum, dtable):
    at = block_at(b)
    n = n_ref[at, :]
    from_nodes = dot(hits(column(index_row(recv_ref, b)), TILE), dinbound[tile_at(b), :])
    dmessage = (grad_ref[at, :].astype(F32) + from_nodes) * live_of(b, count)
    gain_sum[0:1, :] += jnp.sum(dmessage * n, axis=0, keepdims=True)
    dy = layer_norm_grad(dmessage * gain, n, rstd_ref[at, :]).astype(BF16)
    dz = (dot_nt(dy, w2).astype(BF16).astype(F32) * silu_grad(z_ref[at, :])).astype(BF16)
    dsent = dot_nt(dz, w1s).astype(BF16)
    dy_out[at, :] = dy
    dz_out[at, :] = dz
    dsent_out[at, :] = dsent
    ids = index_row(send_ref, b)
    upper = column(ids) >= 2 * NODES + G
    dsent32 = dsent.astype(F32)
    pair = jnp.concatenate(
        [jnp.where(upper, 0.0, dsent32).astype(BF16), jnp.where(upper, dsent32, 0.0).astype(BF16)],
        axis=1,
    )
    dtable[...] += dot(hits_t(ghost_index(ids), NODES), pair)


def all_edges_backward(count, grad_ref, dinbound, residuals, send_ref, recv_ref, w1s, w2, gain,
                       outs, gain_sum, dtable, ghost_grad_out):
    gain_sum[...] = jnp.zeros_like(gain_sum)
    dtable[...] = jnp.zeros_like(dtable)

    def step(b, carry):
        edges_backward(
            b, count, grad_ref, dinbound, *residuals, send_ref, recv_ref, w1s, w2, gain, *outs,
            gain_sum, dtable
        )
        return carry

    lax.fori_loop(0, BLOCKS, step, 0, unroll=True)
    for s in range(8):
        rows, half = pl.ds((s % 4) * G, G), pl.ds((s // 4) * L, L)
        put_slab(ghost_grad_out, s, dtable[rows, half].astype(BF16))


def after_kernel(part, layer, sent_ref, received_ref, edges_ref, z_ref, dy_ref, dz_ref, dsent_ref,
                 send_ref, recv_ref, w1_ref, edge_grad_ref, *rest):
    if part:
        dw1_in, dw2_in, dlocal_in, dtile_in, sums_ref, partial_ref = rest[:6]
        edge_grad_out, partial_out, packed_out, dw1, dw2, dlocal, dtile = rest[6:]
        dw1[...] = dw1_in[...]
        dw2[...] = dw2_in[...]
        dlocal[...] = dlocal_in[...]
    else:
        edge_grad_out, dw1, dw2, dlocal, dtile = rest
        dw1[...] = jnp.zeros_like(dw1)
        dw2[...] = jnp.zeros_like(dw2)
        dlocal[...] = jnp.zeros_like(dlocal)
    dtile[...] = jnp.zeros_like(dtile)
    w1re = w1_ref[layer, L:, :]

    def step(i, carry):
        b = i + part * PART_BLOCKS
        at = block_at(b)
        z = z_ref[at, :]
        dz = dz_ref[at, :]
        dw2[...] += dot_tn((z * sigmoid(z)).astype(BF16), dy_ref[at, :])
        joined = jnp.concatenate(
            [sent_ref[at, :], received_ref[block_at(i), :], edges_ref[at, :]], axis=1
        )
        dw1[...] += dot_tn(joined, dz)
        back = dot_nt(dz, w1re).astype(BF16)
        grad_at = at if edge_grad_ref.shape[0] == EDGES else block_at(i)
        edge_grad = edge_grad_ref[grad_at, :].astype(F32) + back[:, L:].astype(F32)
        edge_grad_out[block_at(i), :] = edge_grad.astype(edge_grad_out.dtype)
        dtile[...] += dot(hits_t(index_row(recv_ref, b), TILE), back[:, :L])
        ids = index_row(send_ref, b)
        upper = column(ids) >= TILE
        dsent32 = dsent_ref[at, :].astype(F32)
        pair = jnp.concatenate(
            [
                jnp.where(upper, 0.0, dsent32).astype(BF16),
                jnp.where(upper, dsent32, 0.0).astype(BF16),
            ],
            axis=1,
        )
        dlocal[...] += dot(hits_t(local_index(ids), TILE), pair)
        return carry

    lax.fori_loop(0, PART_BLOCKS, step, 0, unroll=True)
    if part:
        partial_out[0:TILE, :] = partial_ref[0:TILE, :] + dtile_in[...] + dlocal[:, :L]
        partial_out[TILE:, :] = partial_ref[TILE:, :] + dtile[...] + dlocal[:, L:]
        gains = sums_ref[512:520, :]
        high = gains.astype(BF16).astype(F32)
        packed_out[0:384, :] = dw1[...].astype(BF16)
        packed_out[384:512, :] = dw2[...].astype(BF16)
        packed_out[512:896, :] = sums_ref[128:512, :].astype(BF16)
        packed_out[896:912, :] = jnp.concatenate([high, gains - high], axis=0).astype(BF16)
        packed_out[912:PACKED, :] = jnp.zeros((PACKED - 912, L), BF16)


def pick_kernel(nodes_ref, ghost_row_ref, *slabs):
    pick(nodes_ref[...], ghost_row_ref, slabs)


def turn_kernel(from_before, same, from_after, left, right):
    left[0] = from_before[0]
    left[1] = same[0]
    left[2] = from_after[0]
    right[0] = from_before[2]
    right[1] = same[1]
    right[2] = from_after[2]


def first_kernel(
    count_ref, nodes_ref, edges_ref, send_ref, recv_ref, ghost_row_ref, w1_ref, w2_ref, g1_ref,
    u1_ref, u2_ref, g2_ref, sent0, z0, sent1, z1, *rest
):
    ghost_refs, rest = rest[:4], rest[4:]
    nodes_out, inbound_out, *slabs = rest[:5]
    outs, (table, inbound) = rest[5:10], rest[10:]
    all_edges_forward(
        count_ref[0, 0], (sent0, z0, sent1, z1), ghost_refs, table, edges_ref, send_ref, recv_ref,
        w1_ref[0, :L, :], w2_ref[0], g1_ref[0:1, :], inbound, outs
    )
    inbound_b = inbound[...].astype(BF16)
    inbound_out[...] = inbound_b
    nodes_next = nodes_forward(nodes_ref[...], inbound_b, u1_ref[0], u2_ref[0], g2_ref[0:1, :])[-1]
    nodes_out[...] = nodes_next
    pick(nodes_next, ghost_row_ref, slabs)


def start_nodes_backward(grad, nodes_b, inbound_b, layer, u1_ref, u2_ref, g2_ref, sums):
    u1, u2, gain = u1_ref[layer], u2_ref[layer], g2_ref[layer : layer + 1, :]
    sums[512:520, :] = jnp.zeros((8, L), F32)
    *saved, nodes_next = nodes_forward(nodes_b, inbound_b, u1, u2, gain)
    through, dinbound = nodes_backward(grad, *saved, u1, u2, gain, sums)
    return nodes_next, grad + through, dinbound


def middle_kernel(
    count_ref, nodes_ref, edges_ref, send_ref, recv_ref, w1_ref, w2_ref, g1_ref, u1_ref, u2_ref,
    g2_ref, node_grad_ref, edge_grad_ref, sent0, z0, sent1, z1, *rest
):
    ghost_refs, rest = rest[:4], rest[4:]
    nodes_out, edges_out, sent_out, z_out, dy_out, dz_out, dsent_out = rest[:7]
    partial_out, sums, *ghost_grad_out = rest[7:12]
    table, inbound, n_all, rstd_all, dinbound, dtable, gain_sum = rest[12:]
    count = count_ref[0, 0]
    w1s, w2, gain = w1_ref[1, :L, :], w2_ref[1], g1_ref[1:2, :]
    all_edges_forward(
        count, (sent0, z0, sent1, z1), ghost_refs, table, edges_ref, send_ref, recv_ref, w1s, w2,
        gain, inbound, (edges_out, sent_out, z_out, n_all, rstd_all)
    )
    nodes_out[...], partial_out[...], dinbound[...] = start_nodes_backward(
        node_grad_ref[...].astype(F32), nodes_ref[...], inbound[...].astype(BF16), 1, u1_ref,
        u2_ref, g2_ref, sums
    )
    all_edges_backward(
        count, edge_grad_ref, dinbound, (z_out, n_all, rstd_all), send_ref, recv_ref, w1s, w2, gain,
        (dy_out, dz_out, dsent_out), gain_sum, dtable, ghost_grad_out
    )
    sums[512:513, :] = gain_sum[0:1, :]


def last_kernel(
    count_ref, nodes_ref, inbound_ref, send_ref, recv_ref, ghost_row_ref, w1_ref, w2_ref, g1_ref,
    u1_ref, u2_ref, g2_ref, partial_ref, edge_grad0_ref, edge_grad1_ref, z_ref, n_ref, rstd_ref,
    *rest
):
    returned_refs, rest = rest[:4], rest[4:]
    dy_out, dz_out, dsent_out, partial_out, sums, *ghost_grad_out = rest[:8]
    dinbound, dtable, gain_sum, edge_grad = rest[8:]
    node_grad = add_returned(partial_ref[...], returned_refs, ghost_row_ref)
    _, partial_out[...], dinbound[...] = start_nodes_backward(
        node_grad.astype(BF16).astype(F32), nodes_ref[...], inbound_ref[...], 0, u1_ref, u2_ref,
        g2_ref, sums
    )
    edge_grad[0:PART, :] = edge_grad0_ref[...]
    edge_grad[PART:, :] = edge_grad1_ref[...]
    all_edges_backward(
        count_ref[0, 0], edge_grad, dinbound, (z_ref, n_ref, rstd_ref), send_ref, recv_ref,
        w1_ref[0, :L, :], w2_ref[0], g1_ref[0:1, :], (dy_out, dz_out, dsent_out), gain_sum, dtable,
        ghost_grad_out
    )
    sums[512:513, :] = gain_sum[0:1, :]


def add_returned(partial, returned_refs, ghost_row_ref):
    row = jnp.concatenate([ghost_row_ref[i, j : j + 1, :] for i, j in OUTER], axis=1)
    returned = jnp.concatenate(arrived(returned_refs), axis=0)
    return partial + dot(hits_t(row, NODES), returned)


def return_kernel(partial_ref, ghost_row_ref, *rest):
    rest[4][...] = add_returned(partial_ref[...], rest[:4], ghost_row_ref)


def call(kernel, name, outs, scratch, scalars, flops, *args):
    vmem = pl.BlockSpec(memory_space=pltpu.VMEM)
    smem = pl.BlockSpec(memory_space=pltpu.SMEM)
    return pl.pallas_call(
        kernel,
        name=name,
        out_shape=[jax.ShapeDtypeStruct(s, d) for s, d in outs],
        in_specs=[smem] * scalars + [vmem] * (len(args) - scalars),
        out_specs=[vmem] * len(outs),
        scratch_shapes=[pltpu.VMEM(s, d) for s, d in scratch],
        cost_estimate=pl.CostEstimate(flops=flops, bytes_accessed=1 << 20, transcendentals=0),
        compiler_params=pltpu.CompilerParams(vmem_limit_bytes=24 * 1024 * 1024),
    )(*args)


def shifts(axis):
    up = [(i, i + 1) for i in range(lax.axis_size(axis) - 1)]
    return up, [(j, i) for i, j in up]


def exchange(slabs, beside):
    low, same, high = slabs
    up, down = shifts("gx")
    from_before = lax.ppermute(high, "gx", up)
    from_after = lax.ppermute(low, "gx", down)
    first = beside(0, None)
    left, right = call(
        turn_kernel, "turn", [(low.shape, BF16)] * 2, [], 0, 10**6, from_before, same, from_after
    )
    up, down = shifts("gy")
    before = lax.ppermute(right, "gy", up)
    after = lax.ppermute(left, "gy", down)
    second = beside(1, (first, right))
    return (before, from_before, after, from_after), first, second


def sum_over_domains(packed):
    axes = ("gx", "gy")
    sizes = (lax.axis_size("gx"), lax.axis_size("gy"))
    plane, line = planes_and_lines(*sizes)

    def trade(parts, groups):
        return lax.all_to_all(parts, axes, 0, 0, tiled=True, axis_index_groups=groups)

    def copies(part, groups):
        return trade(jnp.broadcast_to(part[None], (len(groups[0]),) + part.shape), groups)

    parts = trade(packed.reshape(len(plane[0]), -1, L), plane)
    mine = jnp.sum(parts.astype(F32), axis=0).astype(BF16)
    mine = jnp.sum(copies(mine, line).astype(F32), axis=0).astype(BF16)
    return copies(mine, plane).reshape(LAYERS, PACKED, L)


def planes_and_lines(rows, columns):
    planes, lines = {}, {}
    for i in range(rows * columns):
        gx, gy = divmod(i, columns)
        y, z_low = divmod(gx, 4)
        z_high, rest = divmod(gy, 8)
        planes.setdefault((z_high, z_low), []).append(i)
        lines.setdefault((y, rest), []).append(i)
    return list(planes.values()), list(lines.values())


def unpack_kernel(total_ref, dw1, dw2, dg1, du1, du2, dg2):
    for i in range(LAYERS):
        dw1[i] = total_ref[i, 0:384, :].astype(F32)
        dw2[i] = total_ref[i, 384:512, :].astype(F32)
        du1[i] = total_ref[i, 512:768, :].astype(F32)
        du2[i] = total_ref[i, 768:896, :].astype(F32)
        gains = total_ref[i, 896:912, :].astype(F32)
        dg1[i : i + 1, :] = gains[0:1, :] + gains[8:9, :]
        dg2[i : i + 1, :] = gains[1:2, :] + gains[9:10, :]


def on_device(
    latents,
    edge_latents,
    senders,
    receivers,
    ghost_rows,
    edge_count,
    node_cotangent,
    edge_cotangent,
    edge_first,
    edge_second,
    edge_scale,
    node_first,
    node_second,
    node_scale,
):
    nodes0 = latents[0, 0]
    edges0 = edge_latents[0, 0]
    ids = senders[0]
    targets = receivers[0]
    grow = ghost_rows[0, 0]
    weights = (edge_first, edge_second, edge_scale, node_first, node_second, node_scale)

    node_b = ((NODES, L), BF16)
    node_f = ((NODES, L), F32)
    edge_b = ((EDGES, L), BF16)
    edge_f = ((EDGES, L), F32)
    part_b = ((PART, L), BF16)
    part_f = ((PART, L), F32)
    slabs_b = [((n, G, L), BF16) for n in (3, 2, 3)]
    packed_b = ((PACKED, L), BF16)
    sums_f = ((520, L), F32)
    pair_b = ((NODES, 2 * L), BF16)
    pair_f = ((NODES, 2 * L), F32)
    gain_f = ((8, L), F32)
    dw1_f = ((3 * L, L), F32)
    dw2_f = ((L, L), F32)
    dlocal_f = ((TILE, 2 * L), F32)
    dtile_f = ((TILE, L), F32)

    def before(layer, nodes, edges):
        def part_of(part, wait):
            node_arg = nodes
            if wait is not None:
                node_arg, _ = lax.optimization_barrier((nodes, wait))
            return call(
                functools.partial(before_kernel, part, layer), f"before{layer}{part}",
                [part_b, part_b, part_f], [], 0, 2 * 10**9, node_arg, edges, ids, targets,
                edge_first
            )

        return part_of

    def after(layer, sent, received, edges, z, dy, dz, dsent, edge_grads, out, sums, partial):
        def part_of(part, wait):
            dy_arg, extra = dy, ()
            if part:
                dy_arg, _ = lax.optimization_barrier((dy, wait[1]))
                extra = (*wait[0][1:], sums, partial)
            outs = [(part_b[0], out)]
            outs += [node_f, packed_b] if part else [dw1_f, dw2_f, dlocal_f, dtile_f]
            return call(
                functools.partial(after_kernel, part, layer), f"after{layer}{part}", outs,
                [dw1_f, dw2_f, dlocal_f, dtile_f] if part else [], 0, 2 * 10**9, sent,
                received[part], edges, z, dy_arg, dz, dsent, ids, targets, edge_first, edge_grads[part],
                *extra
            )

        return part_of

    picked = call(pick_kernel, "pick", slabs_b, [], 0, 10**8, nodes0, grow)
    ghosts, a0, a1 = exchange(picked, before(0, nodes0, edges0))
    nodes1, inbound, *picked, edges1, sent_0, z_0, n_0, rstd_0 = call(
        first_kernel, "first", [node_b, node_b, *slabs_b, edge_b, edge_b, edge_f, edge_f, edge_f],
        [pair_b, node_f], 1, 4 * 10**9, edge_count, nodes0, edges0, ids, targets, grow, *weights,
        a0[0], a0[2], a1[0], a1[2], *ghosts
    )
    received_0 = (a0[1], a1[1])
    ghosts, a0, a1 = exchange(picked, before(1, nodes1, edges1))
    received_1 = (a0[1], a1[1])
    nodes2, edges2, sent_1, z_1, dy, dz, dsent, partial, sums, *ghost_grad = call(
        middle_kernel, "middle",
        [node_b, edge_b, edge_b, edge_f, edge_b, edge_b, edge_b, node_f, sums_f, *slabs_b],
        [pair_b, node_f, edge_f, edge_f, node_b, pair_f, gain_f], 1, 8 * 10**9, edge_count, nodes1,
        edges1, ids, targets, *weights, node_cotangent[0, 0], edge_cotangent[0, 0], a0[0], a0[2],
        a1[0], a1[2], *ghosts
    )
    returned, c0, c1 = exchange(
        ghost_grad,
        after(1, sent_1, received_1, edges1, z_1, dy, dz, dsent, (edge_cotangent[0, 0],) * 2, BF16,
              sums, partial),
    )
    edge_grad0, (edge_grad1, partial, packed1) = c0[0], c1
    dy, dz, dsent, partial, sums, *ghost_grad = call(
        last_kernel, "last", [edge_b, edge_b, edge_b, node_f, sums_f, *slabs_b],
        [node_b, pair_f, gain_f, edge_b], 1, 4 * 10**9, edge_count, nodes0, inbound, ids, targets,
        grow, *weights, partial, edge_grad0, edge_grad1, z_0, n_0, rstd_0, *returned
    )
    returned, c0, c1 = exchange(
        ghost_grad,
        after(0, sent_0, received_0, edges0, z_0, dy, dz, dsent, (edge_grad0, edge_grad1), F32, sums,
              partial),
    )
    edge_grad0, (edge_grad1, partial, packed0) = c0[0], c1
    (node_grad,) = call(
        return_kernel, "returned", [node_f], [], 0, 10**8, partial, grow, *returned
    )
    total = sum_over_domains(jnp.concatenate([packed0, packed1], axis=0))
    grads = call(
        unpack_kernel, "unpack", [((LAYERS,) + w.shape[1:], F32) for w in weights], [], 0, 10**6,
        total
    )
    return (
        nodes2[None, None],
        edges2[None, None],
        node_grad[None, None],
        jnp.concatenate([edge_grad0, edge_grad1], axis=0)[None, None],
        *grads,
    )


def solution(mesh):
    domain = P("gx", "gy", None, None)
    placed = (
        domain,
        domain,
        P("gx", "gy", None),
        P("gx", "gy", None),
        P("gx", "gy", None, None, None),
        P("gx", "gy"),
        domain,
        domain,
        P(),
        P(),
        P(),
        P(),
        P(),
        P(),
    )
    return jax.shard_map(
        on_device,
        mesh=mesh,
        in_specs=placed,
        out_specs=(domain, domain, domain, domain, P(), P(), P(), P(), P(), P()),
        check_vma=False,
    )
```

time: 215 us -> 176 us (0.82)
  blocking collectives: 0 us -> 42.9 us
  starting transfers between devices: 95.5 us -> 57.3 us
  waiting for transfers between devices: 50.7 us -> 28.2 us
  Pallas kernels: 54.3 us -> 36.4 us
  other arithmetic: 4.13 us -> 1.6 us
    all_to_all x0 -> x1, blocking collectives: none -> 42.9 us  [trade(): lax.all_to_all(parts, axes, 0, 0, tiled=True, axis_index_groups=groups)]
    all_to_all x2, starting transfers between devices: 49.1 us -> 12.9 us  [trade(): lax.all_to_all(parts, axes, 0, 0, tiled=True, axis_index_groups=groups)]
    all_to_all x2, waiting for transfers between devices: 30.3 us -> 11 us  [trade(): lax.all_to_all(parts, axes, 0, 0, tiled=True, axis_index_groups=groups)]
    pallas_call x5 -> x18, Pallas kernels: 54.3 us -> 36.4 us  [call(): pl.pallas_call(kernel, name=name, out_shape=[jax.ShapeDtypeStruct(s, d) f...]
    ppermute x4, waiting for transfers between devices: 17 us -> 2.02 us  [exchange(): after = lax.ppermute(left, 'gy', down)]
    ppermute x4, waiting for transfers between devices: 0.1 us -> 14.6 us  [exchange(): from_after = lax.ppermute(low, 'gx', down)]
    ppermute x4, starting transfers between devices: 20 us -> 15 us  [exchange(): from_before = lax.ppermute(high, 'gx', up)]
    unnamed x38 -> x31, local copies, waits for them, and re-layouts: 1.17 us -> 5.24 us
  transfers between devices with their start and end apart: 18 -> 18, of which waited for: 9 -> 9; matrix products, arithmetic and copies ran while one was open for 3% -> 1% of each run, Pallas kernels for 1% -> 7%
where the time goes in v2:
time: 176 us; the launch traced here: 175 us
  starting transfers between devices  57.3 us (33%)
  blocking collectives  42.9 us (24%)
  Pallas kernels  36.4 us (21%)
  waiting for transfers between devices  28.2 us (16%)
  local copies, waits for them, and re-layouts  6.83 us (4%)
    all_to_all x1, blocking collectives, trade(): lax.all_to_all(parts, axes, 0, 0, tiled=True, axis_index_groups=groups)  42.9 us
    pallas_call x18, Pallas kernels, call(): pl.pallas_call(kernel, name=name, out_shape=[jax.ShapeDtypeStruct(s, d) f...  36.4 us
    ppermute x4, starting transfers between devices, exchange(): before = lax.ppermute(right, 'gy', up)  15.5 us
    ppermute x4, starting transfers between devices, exchange(): from_before = lax.ppermute(high, 'gx', up)  15 us
    ppermute x4, waiting for transfers between devices, exchange(): from_after = lax.ppermute(low, 'gx', down)  14.6 us
    all_to_all x2, starting transfers between devices, trade(): lax.all_to_all(parts, axes, 0, 0, tiled=True, axis_index_groups=groups)  12.9 us
    all_to_all x2, waiting for transfers between devices, trade(): lax.all_to_all(parts, axes, 0, 0, tiled=True, axis_index_groups=groups)  11 us
    ppermute x4, starting transfers between devices, exchange(): after = lax.ppermute(left, 'gy', down)  8.16 us
  transfers between devices with their start and end apart: 18, of which 9 were waited for; matrix products, arithmetic and copies ran while one was open for 1% of the time, Pallas kernels for 7%

profile of v2, /device:TPU:1, one launch (start us, length us, event | category | flops | bytes accessed | tf_op | source)
XLA Modules:
  0.0 174.9 jit_solution(954113761739668120)
XLA Ops:
  0.6 0.7 copy.26
  1.3 0.9 copy-done.8
  2.2 0.5 pick.1
  2.7 4.4 %collective-permute-start = (bf16[3,128,128]{2,1,0:T(8,128)(2,1)S(1)}, bf16[3,128,128]{2,1,0:T(8,128)(2,1)S(1)}, u32[]{:S(2)}, u32[]{:S(2)}) collective-permute-start(bf16[3,128,128]{2,1,0:T(8,128)(2,1)S(1)} %get-tuple-element.92), channel_id=1, source_target_pairs={{0,16},{16,32},{32,48},{48,64},{64,80},{80,96},{96,112},{112,128},... | collective-permute-start | bytes 294920 | tf_op jit(solution)/shard_map/ppermute | solution.py:440
  7.1 1.3 collective-permute-start.1
  9.1 0.0 copy-start.1
  9.1 1.2 copy-done.1
  10.3 0.9 copy-done.3
  11.2 0.7 copy-done.5
  11.9 0.7 copy-done.6
  12.7 1.2 before00.1
  13.8 0.0 collective-permute-done.from_before.rest_1_
  13.8 1.3 collective-permute-done.1.from_after.rest_3_
  15.2 2.4 %collective-permute-start.3 = (bf16[3,128,128]{2,1,0:T(8,128)(2,1)S(1)}, bf16[3,128,128]{2,1,0:T(8,128)(2,1)S(1)}, u32[]{:S(2)}, u32[]{:S(2)}) collective-permute-start(bf16[3,128,128]{2,1,0:T(8,128)(2,1)S(1)} %get-tuple-element.99), channel_id=1, source_target_pairs={{1,0},{2,1},{3,2},{4,3},{5,4},{6,5},{7,6},{8,7},{9,8},{10,9},{11,1... | collective-permute-start | bytes 294920 | tf_op jit(solution)/shard_map/ppermute | solution.py:448
  17.6 3.2 %collective-permute-start.2 = (bf16[3,128,128]{2,1,0:T(8,128)(2,1)S(1)}, bf16[3,128,128]{2,1,0:T(8,128)(2,1)S(1)}, u32[]{:S(2)}, u32[]{:S(2)}) collective-permute-start(bf16[3,128,128]{2,1,0:T(8,128)(2,1)S(1)} %get-tuple-element.95), channel_id=1, source_target_pairs={{0,1},{1,2},{2,3},{3,4},{4,5},{5,6},{6,7},{7,8},{8,9},{9,10},{10,1... | collective-permute-start | bytes 294920 | tf_op jit(solution)/shard_map/ppermute | solution.py:447
  20.8 0.0 copy-start.10
  20.8 0.0 copy-start.11
  20.8 0.0 copy-start.12
  20.8 0.0 copy-start.13
  20.8 0.0 copy-start.14
  20.8 1.2 before01.1
  22.0 0.0 collective-permute-done.3.rest_2_
  22.0 0.4 collective-permute-done.2.rest_0_
  22.4 6.0 %first.1 = (bf16[512,128]{1,0:T(8,128)(2,1)S(1)}, bf16[512,128]{1,0:T(8,128)(2,1)S(1)}, bf16[3,128,128]{2,1,0:T(8,128)(2,1)S(1)}, bf16[2,128,128]{2,1,0:T(8,128)...) custom-call(s32[1,1]{1,0:T(1,128)S(6)} %copy.27.count_ref, ...), custom_call_target="tpu_custom_call" | custom-call | flops 4000000000 | bytes 1048576 | tf_op jit(solution)/shard_map/first/pallas_call | solution.py:420
  28.4 3.3 %collective-permute-start.4 = (bf16[3,128,128]{2,1,0:T(8,128)(2,1)S(1)}, bf16[3,128,128]{2,1,0:T(8,128)(2,1)S(1)}, u32[]{:S(2)}, u32[]{:S(2)}) collective-permute-start(bf16[3,128,128]{2,1,0:T(8,128)(2,1)S(1)} %get-tuple-element.105), channel_id=1, source_target_pairs={{0,16},{16,32},{32,48},{48,64},{64,80},{80,96},{96,112},{112,128},... | collective-permute-start | bytes 294920 | tf_op jit(solution)/shard_map/ppermute | solution.py:440
  31.7 1.3 collective-permute-start.5
  33.0 1.2 before10.1
  34.2 0.0 collective-permute-done.4.from_before.rest_1_
  34.2 5.8 %collective-permute-done.5.from_after.rest_3_ = bf16[3,128,128]{2,1,0:T(8,128)(2,1)S(1)} collective-permute-done((bf16[3,128,128]{2,1,0:T(8,128)(2,1)S(1)}, bf16[3,128,128]{2,1,0:T(8,128)(2,1)S(1)}, u32[]{:S(2)}, u32[]{:S(2)}) %collective-permute-start.5) | collective-permute-done | bytes 98336 | tf_op jit(solution)/shard_map/ppermute | solution.py:441
  40.1 1.9 %collective-permute-start.7 = (bf16[3,128,128]{2,1,0:T(8,128)(2,1)S(1)}, bf16[3,128,128]{2,1,0:T(8,128)(2,1)S(1)}, u32[]{:S(2)}, u32[]{:S(2)}) collective-permute-start(bf16[3,128,128]{2,1,0:T(8,128)(2,1)S(1)} %get-tuple-element.112), channel_id=1, source_target_pairs={{1,0},{2,1},{3,2},{4,3},{5,4},{6,5},{7,6},{8,7},{9,8},{10,9},{11,1... | collective-permute-start | bytes 294920 | tf_op jit(solution)/shard_map/ppermute | solution.py:448
  42.0 4.6 %collective-permute-start.6 = (bf16[3,128,128]{2,1,0:T(8,128)(2,1)S(1)}, bf16[3,128,128]{2,1,0:T(8,128)(2,1)S(1)}, u32[]{:S(2)}, u32[]{:S(2)}) collective-permute-start(bf16[3,128,128]{2,1,0:T(8,128)(2,1)S(1)} %get-tuple-element.108), channel_id=1, source_target_pairs={{0,1},{1,2},{2,3},{3,4},{4,5},{5,6},{6,7},{7,8},{8,9},{9,10},{10,1... | collective-permute-start | bytes 294920 | tf_op jit(solution)/shard_map/ppermute | solution.py:447
  46.6 0.0 copy-start
  46.6 0.0 copy-start.7
  46.6 1.2 before11.1
  47.8 0.2 collective-permute-done.6.rest_0_
  48.0 9.8 %middle.1 = (bf16[512,128]{1,0:T(8,128)(2,1)}, bf16[4096,128]{1,0:T(8,128)(2,1)}, bf16[4096,128]{1,0:T(8,128)(2,1)S(1)}, f32[4096,128]{1,0:T(8,128)S(1)}, bf16[4...) custom-call(s32[1,1]{1,0:T(1,128)S(6)} %copy.27.count_ref, ...), custom_call_target="tpu_custom_call" | custom-call | flops 8000000000 | bytes 1048576 | tf_op jit(solution)/shard_map/middle/pallas_call | solution.py:420
  57.8 3.3 %collective-permute-start.8 = (bf16[3,128,128]{2,1,0:T(8,128)(2,1)S(1)}, bf16[3,128,128]{2,1,0:T(8,128)(2,1)S(1)}, u32[]{:S(2)}, u32[]{:S(2)}) collective-permute-start(bf16[3,128,128]{2,1,0:T(8,128)(2,1)S(1)} %get-tuple-element.123), channel_id=1, source_target_pairs={{0,16},{16,32},{32,48},{48,64},{64,80},{80,96},{96,112},{112,128},... | collective-permute-start | bytes 294920 | tf_op jit(solution)/shard_map/ppermute | solution.py:440
  61.0 1.5 collective-permute-start.9
  62.6 2.0 %after10.1 = (bf16[2048,128]{1,0:T(8,128)(2,1)S(1)}, f32[384,128]{1,0:T(8,128)S(1)}, f32[128,128]{1,0:T(8,128)S(1)}, f32[256,256]{1,0:T(8,128)S(1)}, f32[256,128]{1,0:T(8,128)S(1)}) custom-call(bf16[4096,128]{1,0:T(8,128)(2,1)S(1)} %get-tuple-element.119.sent_ref, bf16[2048,128]{1,0:T(8,128)(2,1)S(1)} %get-tuple-element.104.received_ref, ...), custom_call_target="tpu_custom_call" | custom-call | flops 2000000000 | bytes 1048576 | tf_op jit(solution)/shard_map/after10/pallas_call | solution.py:420
  64.6 4.3 %collective-permute-done.9.from_after.rest_3_ = bf16[3,128,128]{2,1,0:T(8,128)(2,1)S(1)} collective-permute-done((bf16[3,128,128]{2,1,0:T(8,128)(2,1)S(1)}, bf16[3,128,128]{2,1,0:T(8,128)(2,1)S(1)}, u32[]{:S(2)}, u32[]{:S(2)}) %collective-permute-start.9) | collective-permute-done | bytes 98336 | tf_op jit(solution)/shard_map/ppermute | solution.py:441
  68.9 5.0 %collective-permute-start.10 = (bf16[3,128,128]{2,1,0:T(8,128)(2,1)S(1)}, bf16[3,128,128]{2,1,0:T(8,128)(2,1)S(1)}, u32[]{:S(2)}, u32[]{:S(2)}) collective-permute-start(bf16[3,128,128]{2,1,0:T(8,128)(2,1)S(1)} %get-tuple-element.126), channel_id=1, source_target_pairs={{0,1},{1,2},{2,3},{3,4},{4,5},{5,6},{6,7},{7,8},{8,9},{9,10},{10,1... | collective-permute-start | bytes 294920 | tf_op jit(solution)/shard_map/ppermute | solution.py:447
  73.9 1.9 %collective-permute-start.11 = (bf16[3,128,128]{2,1,0:T(8,128)(2,1)S(1)}, bf16[3,128,128]{2,1,0:T(8,128)(2,1)S(1)}, u32[]{:S(2)}, u32[]{:S(2)}) collective-permute-start(bf16[3,128,128]{2,1,0:T(8,128)(2,1)S(1)} %get-tuple-element.141), channel_id=1, source_target_pairs={{1,0},{2,1},{3,2},{4,3},{5,4},{6,5},{7,6},{8,7},{9,8},{10,9},{11,1... | collective-permute-start | bytes 294920 | tf_op jit(solution)/shard_map/ppermute | solution.py:448
  75.8 0.0 copy-start.9
  75.9 2.0 %after11.1 = (bf16[2048,128]{1,0:T(8,128)(2,1)S(1)}, f32[512,128]{1,0:T(8,128)S(1)}, bf16[1024,128]{1,0:T(8,128)(2,1)S(1)}) custom-call(bf16[4096,128]{1,0:T(8,128)(2,1)S(1)} %get-tuple-element.119.sent_ref, bf16[2048,128]{1,0:T(8,128)(2,1)S(1)} %get-tuple-element.120.received_ref, bf16[4096,128]{1,0:T(8,128)(2,1)S(1)} %get-tuple-element.101.edges_ref, ...), custom_call_target="tpu_custom_call" | custom-call | flops 2000000000 | bytes 1048576 | tf_op jit(solution)/shard_map/after11/pallas_call | solution.py:420
  77.8 2.0 %collective-permute-done.11.rest_2_ = bf16[3,128,128]{2,1,0:T(8,128)(2,1)S(1)} collective-permute-done((bf16[3,128,128]{2,1,0:T(8,128)(2,1)S(1)}, bf16[3,128,128]{2,1,0:T(8,128)(2,1)S(1)}, u32[]{:S(2)}, u32[]{:S(2)}) %collective-permute-start.11) | collective-permute-done | bytes 98336 | tf_op jit(solution)/shard_map/ppermute | solution.py:448
  79.9 5.4 %last.1 = (bf16[4096,128]{1,0:T(8,128)(2,1)S(1)}, bf16[4096,128]{1,0:T(8,128)(2,1)S(1)}, bf16[4096,128]{1,0:T(8,128)(2,1)S(1)}, f32[512,128]{1,0:T(8,128)S(1)}, ...) custom-call(s32[1,1]{1,0:T(1,128)S(6)} %copy.27.count_ref, ...), custom_call_target="tpu_custom_call" | custom-call | flops 4000000000 | bytes 1048576 | tf_op jit(solution)/shard_map/last/pallas_call | solution.py:420
  85.2 4.1 %collective-permute-start.12 = (bf16[3,128,128]{2,1,0:T(8,128)(2,1)S(1)}, bf16[3,128,128]{2,1,0:T(8,128)(2,1)S(1)}, u32[]{:S(2)}, u32[]{:S(2)}) collective-permute-start(bf16[3,128,128]{2,1,0:T(8,128)(2,1)S(1)} %get-tuple-element.143), channel_id=1, source_target_pairs={{0,16},{16,32},{32,48},{48,64},{64,80},{80,96},{96,112},{112,128},... | collective-permute-start | bytes 294920 | tf_op jit(solution)/shard_map/ppermute | solution.py:440
  89.3 1.6 collective-permute-start.13
  90.9 2.0 %after00.1 = (f32[2048,128]{1,0:T(8,128)S(1)}, f32[384,128]{1,0:T(8,128)S(1)}, f32[128,128]{1,0:T(8,128)S(1)}, f32[256,256]{1,0:T(8,128)S(1)}, f32[256,128]{1,0:T(8,128)S(1)}) custom-call(bf16[4096,128]{1,0:T(8,128)(2,1)S(1)} %get-tuple-element.115.sent_ref, bf16[2048,128]{1,0:T(8,128)(2,1)S(1)} %get-tuple-element.91.received_ref, ...), custom_call_target="tpu_custom_call" | custom-call | flops 2000000000 | bytes 1048576 | tf_op jit(solution)/shard_map/after00/pallas_call | solution.py:420
  92.9 3.1 %collective-permute-done.13.from_after.rest_3_ = bf16[3,128,128]{2,1,0:T(8,128)(2,1)S(1)} collective-permute-done((bf16[3,128,128]{2,1,0:T(8,128)(2,1)S(1)}, bf16[3,128,128]{2,1,0:T(8,128)(2,1)S(1)}, u32[]{:S(2)}, u32[]{:S(2)}) %collective-permute-start.13) | collective-permute-done | bytes 98336 | tf_op jit(solution)/shard_map/ppermute | solution.py:441
  96.0 2.0 %after01.1 = (f32[2048,128]{1,0:T(8,128)S(1)}, f32[512,128]{1,0:T(8,128)S(1)}, bf16[1024,128]{1,0:T(8,128)(2,1)S(1)}) custom-call(bf16[4096,128]{1,0:T(8,128)(2,1)S(1)} %get-tuple-element.115.sent_ref, bf16[2048,128]{1,0:T(8,128)(2,1)S(1)} %get-tuple-element.116.received_ref, bf16[4096,128]{1,0:T(8,128)(2,1)S(1)} %bitcast.23, ...), custom_call_target="tpu_custom_call" | custom-call | flops 2000000000 | bytes 1048576 | tf_op jit(solution)/shard_map/after01/pallas_call | solution.py:420
  98.1 42.9 %all_to_all.15 = bf16[32,64,128]{2,1,0:T(8,128)(2,1)S(1)} all-to-all(bf16[32,64,128]{2,1,0:T(8,128)(2,1)S(1)} %bitcast.57), channel_id=1, replica_groups={{0,1,2,3,4,5,6,7,64,65,66,67,68,69,70,71,128,129,130,131,132,133,134,13..., dimensions={0} | all-to-all | bytes 1048576 | tf_op jit(solution)/shard_map/all_to_all | solution.py:459
  141.0 0.1 reduce_sum.24
  141.1 0.7 broadcast_in_dim.28
  141.8 5.2 %all-to-all-start.1 = ((bf16[8,64,128]{2,1,0:T(8,128)(2,1)}), bf16[8,64,128]{2,1,0:T(8,128)(2,1)S(1)}, u32[]{:S(2)}, u32[]{:S(2)}) async-start(bf16[8,64,128]{2,1,0:T(8,128)(2,1)} %broadcast_in_dim.28), calls=%async_computation.1 | async-start | bytes 262144 | tf_op jit(solution)/shard_map/all_to_all | solution.py:459
  146.9 2.8 %collective-permute-start.14 = (bf16[3,128,128]{2,1,0:T(8,128)(2,1)S(1)}, bf16[3,128,128]{2,1,0:T(8,128)(2,1)S(1)}, u32[]{:S(2)}, u32[]{:S(2)}) collective-permute-start(bf16[3,128,128]{2,1,0:T(8,128)(2,1)S(1)} %get-tuple-element.146), channel_id=1, source_target_pairs={{0,1},{1,2},{2,3},{3,4},{4,5},{5,6},{6,7},{7,8},{8,9},{9,10},{10,1... | collective-permute-start | bytes 294920 | tf_op jit(solution)/shard_map/ppermute | solution.py:447
  149.7 1.9 %collective-permute-start.15 = (bf16[3,128,128]{2,1,0:T(8,128)(2,1)S(1)}, bf16[3,128,128]{2,1,0:T(8,128)(2,1)S(1)}, u32[]{:S(2)}, u32[]{:S(2)}) collective-permute-start(bf16[3,128,128]{2,1,0:T(8,128)(2,1)S(1)} %get-tuple-element.157), channel_id=1, source_target_pairs={{1,0},{2,1},{3,2},{4,3},{5,4},{6,5},{7,6},{8,7},{9,8},{10,9},{11,1... | collective-permute-start | bytes 294920 | tf_op jit(solution)/shard_map/ppermute | solution.py:448
  151.6 2.0 %all-to-all-done.1 = bf16[8,64,128]{2,1,0:T(8,128)(2,1)S(1)} async-done(((bf16[8,64,128]{2,1,0:T(8,128)(2,1)}), bf16[8,64,128]{2,1,0:T(8,128)(2,1)S(1)}, u32[]{:S(2)}, u32[]{:S(2)}) %all-to-all-start.1) | async-done | bytes 131104 | tf_op jit(solution)/shard_map/all_to_all | solution.py:459
  153.7 0.9 broadcast_in_dim.29
  154.6 7.8 %all-to-all-start.2 = ((bf16[32,64,128]{2,1,0:T(8,128)(2,1)}), bf16[32,64,128]{2,1,0:T(8,128)(2,1)S(1)}, u32[]{:S(2)}, u32[]{:S(2)}) async-start(bf16[32,64,128]{2,1,0:T(8,128)(2,1)} %broadcast_in_dim.29), calls=%async_computation.2 | async-start | bytes 1048576 | tf_op jit(solution)/shard_map/all_to_all | solution.py:459
  162.4 1.5 maximum_bitcast_fusion
  163.9 1.1 returned.1
  165.0 8.9 %all-to-all-done.2 = bf16[32,64,128]{2,1,0:T(8,128)(2,1)S(1)} async-done(((bf16[32,64,128]{2,1,0:T(8,128)(2,1)}), bf16[32,64,128]{2,1,0:T(8,128)(2,1)S(1)}, u32[]{:S(2)}, u32[]{:S(2)}) %all-to-all-start.2) | async-done | bytes 524320 | tf_op jit(solution)/shard_map/all_to_all | solution.py:459
  173.9 0.9 unpack.1
  (28 shorter events, 0.2 us)
Async XLA Ops:
  1.3 0.9 copy-start.8
  2.7 11.1 %collective-permute-start = (bf16[3,128,128]{2,1,0:T(8,128)(2,1)S(1)}, bf16[3,128,128]{2,1,0:T(8,128)(2,1)S(1)}, u32[]{:S(2)}, u32[]{:S(2)}) collective-permute-start(bf16[3,128,128]{2,1,0:T(8,128)(2,1)S(1)} %get-tuple-element.92), channel_id=1, source_target_pairs={{0,16},{16,32},{32,48},{48,64},{64,80},{80,96},{96,112},{112,128},... | collective-permute-start | bytes 294920 | tf_op jit(solution)/shard_map/ppermute | solution.py:440
  7.1 8.1 %collective-permute-start.1 = (bf16[3,128,128]{2,1,0:T(8,128)(2,1)S(1)}, bf16[3,128,128]{2,1,0:T(8,128)(2,1)S(1)}, u32[]{:S(2)}, u32[]{:S(2)}) collective-permute-start(bf16[3,128,128]{2,1,0:T(8,128)(2,1)S(1)} %get-tuple-element.94), channel_id=1, source_target_pairs={{16,0},{32,16},{48,32},{64,48},{80,64},{96,80},{112,96},{128,112},... | collective-permute-start | bytes 294920 | tf_op jit(solution)/shard_map/ppermute | solution.py:441
  9.1 1.2 copy-start.1
  10.3 0.9 copy-start.3
  11.2 0.7 copy-start.5
  11.9 0.7 copy-start.6
  12.7 8.1 %copy-start.2 = (bf16[1,1,4096,128]{3,2,1,0:T(8,128)(2,1)S(1)}, bf16[1,1,4096,128]{3,2,1,0:T(8,128)(2,1)}, u32[]{:S(2)}) copy-start(bf16[1,1,4096,128]{3,2,1,0:T(8,128)(2,1)} %param.15) | copy-start | bytes 3145732
  15.2 6.8 %collective-permute-start.3 = (bf16[3,128,128]{2,1,0:T(8,128)(2,1)S(1)}, bf16[3,128,128]{2,1,0:T(8,128)(2,1)S(1)}, u32[]{:S(2)}, u32[]{:S(2)}) collective-permute-start(bf16[3,128,128]{2,1,0:T(8,128)(2,1)S(1)} %get-tuple-element.99), channel_id=1, source_target_pairs={{1,0},{2,1},{3,2},{4,3},{5,4},{6,5},{7,6},{8,7},{9,8},{10,9},{11,1... | collective-permute-start | bytes 294920 | tf_op jit(solution)/shard_map/ppermute | solution.py:448
  17.6 4.8 %collective-permute-start.2 = (bf16[3,128,128]{2,1,0:T(8,128)(2,1)S(1)}, bf16[3,128,128]{2,1,0:T(8,128)(2,1)S(1)}, u32[]{:S(2)}, u32[]{:S(2)}) collective-permute-start(bf16[3,128,128]{2,1,0:T(8,128)(2,1)S(1)} %get-tuple-element.95), channel_id=1, source_target_pairs={{0,1},{1,2},{2,3},{3,4},{4,5},{5,6},{6,7},{7,8},{8,9},{9,10},{10,1... | collective-permute-start | bytes 294920 | tf_op jit(solution)/shard_map/ppermute | solution.py:447
  20.8 1.6 copy-start.10
  20.8 1.6 copy-start.11
  20.8 1.6 copy-start.12
  20.8 1.6 copy-start.13
  20.8 1.6 copy-start.14
  28.4 5.8 %collective-permute-start.4 = (bf16[3,128,128]{2,1,0:T(8,128)(2,1)S(1)}, bf16[3,128,128]{2,1,0:T(8,128)(2,1)S(1)}, u32[]{:S(2)}, u32[]{:S(2)}) collective-permute-start(bf16[3,128,128]{2,1,0:T(8,128)(2,1)S(1)} %get-tuple-element.105), channel_id=1, source_target_pairs={{0,16},{16,32},{32,48},{48,64},{64,80},{80,96},{96,112},{112,128},... | collective-permute-start | bytes 294920 | tf_op jit(solution)/shard_map/ppermute | solution.py:440
  31.7 8.3 %collective-permute-start.5 = (bf16[3,128,128]{2,1,0:T(8,128)(2,1)S(1)}, bf16[3,128,128]{2,1,0:T(8,128)(2,1)S(1)}, u32[]{:S(2)}, u32[]{:S(2)}) collective-permute-start(bf16[3,128,128]{2,1,0:T(8,128)(2,1)S(1)} %get-tuple-element.107), channel_id=1, source_target_pairs={{16,0},{32,16},{48,32},{64,48},{80,64},{96,80},{112,96},{128,112},... | collective-permute-start | bytes 294920 | tf_op jit(solution)/shard_map/ppermute | solution.py:441
  40.1 7.7 %collective-permute-start.7 = (bf16[3,128,128]{2,1,0:T(8,128)(2,1)S(1)}, bf16[3,128,128]{2,1,0:T(8,128)(2,1)S(1)}, u32[]{:S(2)}, u32[]{:S(2)}) collective-permute-start(bf16[3,128,128]{2,1,0:T(8,128)(2,1)S(1)} %get-tuple-element.112), channel_id=1, source_target_pairs={{1,0},{2,1},{3,2},{4,3},{5,4},{6,5},{7,6},{8,7},{9,8},{10,9},{11,1... | collective-permute-start | bytes 294920 | tf_op jit(solution)/shard_map/ppermute | solution.py:448
  42.0 6.0 %collective-permute-start.6 = (bf16[3,128,128]{2,1,0:T(8,128)(2,1)S(1)}, bf16[3,128,128]{2,1,0:T(8,128)(2,1)S(1)}, u32[]{:S(2)}, u32[]{:S(2)}) collective-permute-start(bf16[3,128,128]{2,1,0:T(8,128)(2,1)S(1)} %get-tuple-element.108), channel_id=1, source_target_pairs={{0,1},{1,2},{2,3},{3,4},{4,5},{5,6},{6,7},{7,8},{8,9},{9,10},{10,1... | collective-permute-start | bytes 294920 | tf_op jit(solution)/shard_map/ppermute | solution.py:447
  46.6 1.4 copy-start
  46.6 1.4 copy-start.7
  48.0 14.5 %copy-start.4 = (bf16[2,384,128]{2,1,0:T(8,128)(2,1)S(1)}, bf16[2,384,128]{2,1,0:T(8,128)(2,1)}, u32[]{:S(2)}) copy-start(bf16[2,384,128]{2,1,0:T(8,128)(2,1)} %w1_ref.21) | copy-start | bytes 589828
  57.8 6.8 %collective-permute-start.8 = (bf16[3,128,128]{2,1,0:T(8,128)(2,1)S(1)}, bf16[3,128,128]{2,1,0:T(8,128)(2,1)S(1)}, u32[]{:S(2)}, u32[]{:S(2)}) collective-permute-start(bf16[3,128,128]{2,1,0:T(8,128)(2,1)S(1)} %get-tuple-element.123), channel_id=1, source_target_pairs={{0,16},{16,32},{32,48},{48,64},{64,80},{80,96},{96,112},{112,128},... | collective-permute-start | bytes 294920 | tf_op jit(solution)/shard_map/ppermute | solution.py:440
  61.0 7.8 %collective-permute-start.9 = (bf16[3,128,128]{2,1,0:T(8,128)(2,1)S(1)}, bf16[3,128,128]{2,1,0:T(8,128)(2,1)S(1)}, u32[]{:S(2)}, u32[]{:S(2)}) collective-permute-start(bf16[3,128,128]{2,1,0:T(8,128)(2,1)S(1)} %get-tuple-element.125), channel_id=1, source_target_pairs={{16,0},{32,16},{48,32},{64,48},{80,64},{96,80},{112,96},{128,112},... | collective-permute-start | bytes 294920 | tf_op jit(solution)/shard_map/ppermute | solution.py:441
  68.9 11.0 %collective-permute-start.10 = (bf16[3,128,128]{2,1,0:T(8,128)(2,1)S(1)}, bf16[3,128,128]{2,1,0:T(8,128)(2,1)S(1)}, u32[]{:S(2)}, u32[]{:S(2)}) collective-permute-start(bf16[3,128,128]{2,1,0:T(8,128)(2,1)S(1)} %get-tuple-element.126), channel_id=1, source_target_pairs={{0,1},{1,2},{2,3},{3,4},{4,5},{5,6},{6,7},{7,8},{8,9},{9,10},{10,1... | collective-permute-start | bytes 294920 | tf_op jit(solution)/shard_map/ppermute | solution.py:447
  73.9 5.9 %collective-permute-start.11 = (bf16[3,128,128]{2,1,0:T(8,128)(2,1)S(1)}, bf16[3,128,128]{2,1,0:T(8,128)(2,1)S(1)}, u32[]{:S(2)}, u32[]{:S(2)}) collective-permute-start(bf16[3,128,128]{2,1,0:T(8,128)(2,1)S(1)} %get-tuple-element.141), channel_id=1, source_target_pairs={{1,0},{2,1},{3,2},{4,3},{5,4},{6,5},{7,6},{8,7},{9,8},{10,9},{11,1... | collective-permute-start | bytes 294920 | tf_op jit(solution)/shard_map/ppermute | solution.py:448
  75.8 4.0 %copy-start.9 = (bf16[1,1,512,128]{3,2,1,0:T(8,128)(2,1)S(1)}, bf16[1,1,512,128]{3,2,1,0:T(8,128)(2,1)}, u32[]{:S(2)}) copy-start(bf16[1,1,512,128]{3,2,1,0:T(8,128)(2,1)} %param.14) | copy-start | bytes 393220
  85.2 7.6 %collective-permute-start.12 = (bf16[3,128,128]{2,1,0:T(8,128)(2,1)S(1)}, bf16[3,128,128]{2,1,0:T(8,128)(2,1)S(1)}, u32[]{:S(2)}, u32[]{:S(2)}) collective-permute-start(bf16[3,128,128]{2,1,0:T(8,128)(2,1)S(1)} %get-tuple-element.143), channel_id=1, source_target_pairs={{0,16},{16,32},{32,48},{48,64},{64,80},{80,96},{96,112},{112,128},... | collective-permute-start | bytes 294920 | tf_op jit(solution)/shard_map/ppermute | solution.py:440
  89.3 6.7 %collective-permute-start.13 = (bf16[3,128,128]{2,1,0:T(8,128)(2,1)S(1)}, bf16[3,128,128]{2,1,0:T(8,128)(2,1)S(1)}, u32[]{:S(2)}, u32[]{:S(2)}) collective-permute-start(bf16[3,128,128]{2,1,0:T(8,128)(2,1)S(1)} %get-tuple-element.145), channel_id=1, source_target_pairs={{16,0},{32,16},{48,32},{64,48},{80,64},{96,80},{112,96},{128,112},... | collective-permute-start | bytes 294920 | tf_op jit(solution)/shard_map/ppermute | solution.py:441
  141.8 11.9 %all-to-all-start.1 = ((bf16[8,64,128]{2,1,0:T(8,128)(2,1)}), bf16[8,64,128]{2,1,0:T(8,128)(2,1)S(1)}, u32[]{:S(2)}, u32[]{:S(2)}) async-start(bf16[8,64,128]{2,1,0:T(8,128)(2,1)} %broadcast_in_dim.28), calls=%async_computation.1 | async-start | bytes 262144 | tf_op jit(solution)/shard_map/all_to_all | solution.py:459
  146.9 16.9 %collective-permute-start.14 = (bf16[3,128,128]{2,1,0:T(8,128)(2,1)S(1)}, bf16[3,128,128]{2,1,0:T(8,128)(2,1)S(1)}, u32[]{:S(2)}, u32[]{:S(2)}) collective-permute-start(bf16[3,128,128]{2,1,0:T(8,128)(2,1)S(1)} %get-tuple-element.146), channel_id=1, source_target_pairs={{0,1},{1,2},{2,3},{3,4},{4,5},{5,6},{6,7},{7,8},{8,9},{9,10},{10,1... | collective-permute-start | bytes 294920 | tf_op jit(solution)/shard_map/ppermute | solution.py:447
  149.7 14.2 %collective-permute-start.15 = (bf16[3,128,128]{2,1,0:T(8,128)(2,1)S(1)}, bf16[3,128,128]{2,1,0:T(8,128)(2,1)S(1)}, u32[]{:S(2)}, u32[]{:S(2)}) collective-permute-start(bf16[3,128,128]{2,1,0:T(8,128)(2,1)S(1)} %get-tuple-element.157), channel_id=1, source_target_pairs={{1,0},{2,1},{3,2},{4,3},{5,4},{6,5},{7,6},{8,7},{9,8},{10,9},{11,1... | collective-permute-start | bytes 294920 | tf_op jit(solution)/shard_map/ppermute | solution.py:448
  154.6 19.3 %all-to-all-start.2 = ((bf16[32,64,128]{2,1,0:T(8,128)(2,1)}), bf16[32,64,128]{2,1,0:T(8,128)(2,1)S(1)}, u32[]{:S(2)}, u32[]{:S(2)}) async-start(bf16[32,64,128]{2,1,0:T(8,128)(2,1)} %broadcast_in_dim.29), calls=%async_computation.2 | async-start | bytes 1048576 | tf_op jit(solution)/shard_map/all_to_all | solution.py:459
